TPU v7x, 256 devices: a whole 4x4x8 slice. The times are simulated.
256 devices in a mesh: dp: 32 (over y_hi, z, core), tensor: 8 (over y_lo, x).
Axes of the slice: x: 4, y: 4 (y_hi: 2, y_lo: 2; y = y_hi * 2 + y_lo), z: 8, core: 2. Of those that a mesh axis runs over, the one named last changes fastest.
Arguments:
- tokens: bfloat16 [4096, 6144], P('dp', 'tensor'), may hold values from -6 to 6
- weight: bfloat16 [6144, 28672], P('tensor', 'dp'), may hold values from -0.078125 to 0.078125
- factors: float32 [4, 64, 6144], P(None, None, 'tensor'), may hold values from -0.6 to 0.6
- cotangent: bfloat16 [4096, 28672], P('tensor', 'dp'), may hold values from -6 to 6
Outputs:
- projected: bfloat16 [4096, 28672], P('tensor', 'dp')
- grad_tokens: float32 [4096, 6144], P('dp', 'tensor')
- grad_factors: float32 [4, 64, 6144], P(None, None, 'tensor')
All inputs are finite; a program needn't handle non-finite values.
Results may differ from a plain program's by a relative error of at most 0.0049.
Values may be sent and summed in bfloat16 or wider, within the bound.
A program may use at most 128 MiB of HBM per device.

v0:
```python
import jax
import jax.numpy as jnp
from jax import lax
from jax.sharding import PartitionSpec as P

HIGH = lax.Precision.HIGHEST


def swapped(shard, axis, bit):
    return lax.ppermute(shard, axis, [(i, i ^ 1 << bit) for i in range(lax.axis_size(axis))])


def first_forward(field, coeffs, block):
    rows, width = field.shape
    count = width // block
    inputs = field.reshape(rows, count, block)
    added = jnp.einsum("tqk,kqc->tqc", inputs, coeffs.reshape(block, count, block), precision=HIGH)
    return (field + added.reshape(rows, width), inputs)


def first_backward(grad_out, inputs, coeffs, block):
    rows, width = grad_out.shape
    count = width // block
    viewed = grad_out.reshape(rows, count, block)
    grad_coeffs = jnp.einsum("tqk,tqc->kqc", inputs, viewed, precision=HIGH).reshape(block, width)
    grad_inputs = jnp.einsum(
        "tqc,kqc->tqk", viewed, coeffs.reshape(block, count, block), precision=HIGH
    )
    return (grad_out + grad_inputs.reshape(rows, width), grad_coeffs)


def second_forward(field, coeffs, block):
    rows, width = field.shape
    half = block // 2
    count = width // (2 * block)
    viewed = field.reshape(rows, count, 2, 2, half)
    inputs = viewed.transpose(0, 1, 3, 2, 4).reshape(rows, count, 2, block)
    added = jnp.einsum(
        "tqak,kqbaw->tqbaw", inputs, coeffs.reshape(block, count, 2, 2, half), precision=HIGH
    )
    return (field + added.reshape(rows, width), inputs)


def second_backward(grad_out, inputs, coeffs, block):
    rows, width = grad_out.shape
    half = block // 2
    count = width // (2 * block)
    viewed = grad_out.reshape(rows, count, 2, 2, half)
    grad_coeffs = jnp.einsum("tqak,tqbaw->kqbaw", inputs, viewed, precision=HIGH).reshape(
        block, width
    )
    grad_inputs = jnp.einsum(
        "tqbaw,kqbaw->tqak", viewed, coeffs.reshape(block, count, 2, 2, half), precision=HIGH
    )
    grad_inputs = grad_inputs.reshape(rows, count, 2, 2, half).transpose(0, 1, 3, 2, 4)
    return (grad_out + grad_inputs.reshape(rows, width), grad_coeffs)


def lower_side(bit):
    return lax.axis_index("tensor") // (1 << bit) % 2 == 0


def cross_forward(field, coeffs, block, bit):
    rows, width = field.shape
    half = block // 2
    partner = swapped(field, "tensor", bit)
    mine = field.reshape(rows, width // half, half)
    theirs = partner.reshape(rows, width // half, half)
    inputs = jnp.where(
        lower_side(bit), jnp.concatenate([mine, theirs], 2), jnp.concatenate([theirs, mine], 2)
    )
    added = jnp.einsum(
        "thk,khw->thw", inputs, coeffs.reshape(block, width // half, half), precision=HIGH
    )
    return (field + added.reshape(rows, width), inputs)


def cross_backward(grad_out, inputs, coeffs, block, bit):
    rows, width = grad_out.shape
    half = block // 2
    viewed = grad_out.reshape(rows, width // half, half)
    grad_coeffs = jnp.einsum("thk,thw->khw", inputs, viewed, precision=HIGH).reshape(block, width)
    grad_inputs = jnp.einsum(
        "thw,khw->thk", viewed, coeffs.reshape(block, width // half, half), precision=HIGH
    )
    lower = lower_side(bit)
    own_part = jnp.where(lower, grad_inputs[:, :, :half], grad_inputs[:, :, half:])
    other_part = jnp.where(lower, grad_inputs[:, :, half:], grad_inputs[:, :, :half])
    arrived = swapped(other_part.reshape(rows, width), "tensor", bit)
    return (grad_out + own_part.reshape(rows, width) + arrived, grad_coeffs)


def per_device(tokens, weight, factors, cotangent):
    block = factors.shape[1]
    top_bit = lax.axis_size("tensor").bit_length() - 2
    level0 = tokens.astype(jnp.float32)
    level1, inputs0 = first_forward(level0, factors[0], block)
    level2, inputs1 = second_forward(level1, factors[1], block)
    level3, inputs2 = cross_forward(level2, factors[2], block, 0)
    level4, inputs3 = cross_forward(level3, factors[3], block, top_bit)
    rotated = level4.astype(jnp.bfloat16)
    partial_out = jnp.dot(
        lax.all_gather(rotated, "dp", axis=0, tiled=True),
        weight,
        preferred_element_type=jnp.float32,
    )
    projected = lax.psum_scatter(partial_out, "tensor", scatter_dimension=0, tiled=True).astype(
        jnp.bfloat16
    )
    projected, saved = (projected, (inputs0, inputs1, inputs2, inputs3))
    all_cotangent = lax.all_gather(cotangent, "tensor", axis=0, tiled=True)
    back = lax.psum_scatter(
        lax.dot_general(
            all_cotangent, weight, (((1,), (1,)), ((), ())), preferred_element_type=jnp.float32
        ),
        "dp",
        scatter_dimension=0,
        tiled=True,
    )
    grad_now, grad_three = cross_backward(back, saved[3], factors[3], block, top_bit)
    grad_now, grad_two = cross_backward(grad_now, saved[2], factors[2], block, 0)
    grad_now, grad_one = second_backward(grad_now, saved[1], factors[1], block)
    grad_now, grad_zero = first_backward(grad_now, saved[0], factors[0], block)
    stacked = jnp.stack([grad_zero, grad_one, grad_two, grad_three])
    stacked = lax.psum(stacked, "dp")
    return (projected, grad_now, stacked)


def solution(mesh):
    placed = (P("dp", "tensor"), P("tensor", "dp"), P(None, None, "tensor"), P("tensor", "dp"))
    return jax.shard_map(
        per_device,
        mesh=mesh,
        in_specs=placed,
        out_specs=(P("tensor", "dp"), P("dp", "tensor"), P(None, None, "tensor")),
        check_vma=False,
    )
```

profile of v0, /device:TPU:1, one launch (start us, length us, event | category | flops | bytes accessed | tf_op | source)
XLA Modules:
  0.0 815.4 jit_solution(2206288052887867735)
XLA Ops:
  8.0 90.3 %all-gather.5.cloned.1.call-done = bf16[4096,896]{1,0:T(8,128)(2,1)} async-done(((bf16[512,896]{1,0:T(8,128)(2,1)}), bf16[4096,896]{1,0:T(8,128)(2,1)}) %all-gather.5.cloned.1.call-update) | async-done | bytes 7340048 | tf_op jit(solution)/shard_map/all_gather | solution.py:111
  98.3 12.3 %fusion.21 = f32[4096,768]{1,0:T(8,128)} fusion(bf16[4096,896]{1,0:T(8,128)(2,1)} %all-gather.5.cloned.1.call-done, bf16[768,896]{1,0:T(8,128)(2,1)S(1)} %copy-done), kind=kOutput, calls=%fused_computation.38 | convolution fusion | flops 5637144576 | bytes 21299200 | tf_op jit(solution)/shard_map/dot_general | solution.py:113
  115.3 8.9 %collective-permute-done = f32[128,768]{0,1:T(8,128)} collective-permute-done((f32[128,768]{0,1:T(8,128)S(1)}, f32[128,768]{0,1:T(8,128)}, u32[]{:S(2)}, u32[]{:S(2)}) %collective-permute-start) | collective-permute-done | bytes 393248 | tf_op jit(solution)/shard_map/ppermute | solution.py:10
  124.2 2.0 fusion.3
  128.4 8.1 collective-permute-done.1
  136.4 2.3 fusion.1
  138.7 1.7 fusion.4
  140.5 139.1 %reduce-scatter.5.cloned.1.call-done = f32[128,768]{1,0:T(8,128)} async-done(((f32[4096,768]{1,0:T(8,128)}), f32[128,768]{1,0:T(8,128)}) %reduce-scatter.5.cloned.1.call-update) | async-done | bytes 393232 | tf_op jit(solution)/shard_map/reduce_scatter | solution.py:112
  280.8 1.4 convolution_bitcast_fusion.1
  284.7 1.9 copy.77
  286.6 4.6 collective-permute-done.2
  291.2 1.2 add_add_fusion.1
  293.3 2.4 convolution_bitcast_fusion
  296.7 1.9 copy.81
  299.7 3.4 fusion
  303.1 1.9 copy.80
  305.0 3.6 fusion.2
  313.5 2.3 pad_maximum_fusion
  315.8 66.4 %all-gather.3.cloned.1.call-done = bf16[4096,768]{0,1:T(8,128)(2,1)} async-done(((bf16[128,768]{0,1:T(8,128)(2,1)}), bf16[4096,768]{0,1:T(8,128)(2,1)}) %all-gather.3.cloned.1.call-update) | async-done | bytes 6291472 | tf_op jit(solution)/shard_map/all_gather | solution.py:103
  382.2 12.4 %fusion.20 = f32[4096,896]{1,0:T(8,128)} fusion(bf16[4096,768]{0,1:T(8,128)(2,1)} %all-gather.3.cloned.1.call-done, bf16[768,896]{1,0:T(8,128)(2,1)S(1)} %copy-done), kind=kOutput, calls=%fused_computation.37 | convolution fusion | flops 5637144576 | bytes 22347776 | tf_op jit(solution)/shard_map/dot_general | solution.py:102
  396.4 254.1 %all-reduce.2.cloned.1.call-done = f32[4,64,768]{1,2,0:T(8,128)} async-done(((f32[4,64,768]{1,2,0:T(8,128)}), f32[4,64,768]{1,2,0:T(8,128)}) %all-reduce.2.cloned.1.call-update) | async-done | bytes 786448 | tf_op jit(solution)/shard_map/psum | solution.py:125
  650.6 2.7 copy.92
  653.3 153.0 %reduce-scatter.3.cloned.1.call-done = f32[512,896]{1,0:T(8,128)} async-done(((f32[4096,896]{1,0:T(8,128)}), f32[512,896]{1,0:T(8,128)}) %reduce-scatter.3.cloned.1.call-update) | async-done | bytes 1835024 | tf_op jit(solution)/shard_map/reduce_scatter | solution.py:107
  806.3 2.5 convert_element_type.11
  (70 shorter events, 20.7 us)
Async XLA Ops:
  7.2 91.1 %copy-start = (bf16[768,896]{1,0:T(8,128)(2,1)S(1)}, bf16[768,896]{1,0:T(8,128)(2,1)}, u32[]{:S(2)}) copy-start(bf16[768,896]{1,0:T(8,128)(2,1)} %param.5) | copy-start | bytes 4128772
  7.2 91.1 %all-gather.5.cloned.1.call-start = ((), (), s32[]{:S(2)}) async-start(), calls=%async_computation.4 | async-start | bytes 8257536 | tf_op jit(solution)/shard_map/all_gather | solution.py:111
  7.9 271.7 %reduce-scatter.5.cloned.1.call-start = ((), (), s32[]{:S(2)}) async-start(), calls=%async_computation.5 | async-start | bytes 12976128 | tf_op jit(solution)/shard_map/reduce_scatter | solution.py:112
  110.6 1.1 copy-start.9
  110.6 2.1 copy-start.11
  110.6 271.6 %all-gather.3.cloned.1.call-start = ((), (), s32[]{:S(2)}) async-start(), calls=%async_computation.2 | async-start | bytes 6488064 | tf_op jit(solution)/shard_map/all_gather | solution.py:103
  114.0 13.0 %copy-start.8 = (f32[128,768]{0,1:T(8,128)}, f32[128,768]{0,1:T(8,128)S(1)}, u32[]{:S(2)}) copy-start(f32[128,768]{0,1:T(8,128)S(1)} %bitcast_add_fusion.3) | copy-start | bytes 1179652
  114.0 10.2 %collective-permute-start = (f32[128,768]{0,1:T(8,128)S(1)}, f32[128,768]{0,1:T(8,128)}, u32[]{:S(2)}, u32[]{:S(2)}) collective-permute-start(f32[128,768]{0,1:T(8,128)S(1)} %bitcast_add_fusion.3), channel_id=1, source_target_pairs={{0,1},{1,0},{2,3},{3,2},{4,5},{5,4},{6,7},{7,6},{8,9},{9,8},{10,11... | collective-permute-start | bytes 1179656 | tf_op jit(solution)/shard_map/ppermute | solution.py:10
  115.3 13.1 %copy-start.3 = (f32[1,64,768]{1,2,0:T(8,128)}, f32[1,64,768]{1,2,0:T(8,128)S(1)}, u32[]{:S(2)}) copy-start(f32[1,64,768]{1,2,0:T(8,128)S(1)} %copy.74) | copy-start | bytes 589828
  127.0 9.4 %collective-permute-start.1 = (f32[128,768]{0,1:T(8,128)}, f32[128,768]{0,1:T(8,128)}, u32[]{:S(2)}, u32[]{:S(2)}) collective-permute-start(f32[128,768]{0,1:T(8,128)} %bitcast_add_fusion.1), channel_id=1, source_target_pairs={{0,4},{1,5},{2,6},{3,7},{4,0},{5,1},{6,2},{7,3},{8,12},{9,13},{10,... | collective-permute-start | bytes 1179656 | tf_op jit(solution)/shard_map/ppermute | solution.py:10
  140.5 510.1 %all-reduce.2.cloned.1.call-start = ((), (), s32[]{:S(2)}) async-start(), calls=%async_computation.6 | async-start | bytes 3145728 | tf_op jit(solution)/shard_map/psum | solution.py:125
  280.8 2.4 copy-start.4
  282.2 8.9 %copy-start.2 = (f32[128,768]{1,0:T(8,128)S(1)}, f32[128,768]{1,0:T(8,128)}, u32[]{:S(2)}) copy-start(f32[128,768]{1,0:T(8,128)} %reduce-scatter.5.cloned.1.call-done) | copy-start | bytes 1179652
  284.4 6.8 collective-permute-start.2
  292.5 0.7 copy-start.6
  295.7 4.0 copy-start.5
  298.6 10.0 %collective-permute-start.3 = (f32[128,768]{1,0:T(8,128)}, f32[128,768]{1,0:T(8,128)}, u32[]{:S(2)}, u32[]{:S(2)}) collective-permute-start(f32[128,768]{1,0:T(8,128)} %copy.81), channel_id=1, source_target_pairs={{0,1},{1,0},{2,3},{3,2},{4,5},{5,4},{6,7},{7,6},{8,9},{9,8},{10,11... | collective-permute-start | bytes 1179656 | tf_op jit(solution)/shard_map/ppermute | solution.py:10
  305.0 3.6 copy-start.7
  312.4 1.0 copy-start.1
  312.4 1.1 copy-start.10
  315.8 490.5 %reduce-scatter.3.cloned.1.call-start = ((), (), s32[]{:S(2)}) async-start(), calls=%async_computation.3 | async-start | bytes 16515072 | tf_op jit(solution)/shard_map/reduce_scatter | solution.py:107
Sparse Core Ops, SparseCore 0:
  9.8 88.3 all-gather.4
  110.7 168.8 reduce-scatter.4
  282.2 99.9 all-gather.2
  384.7 265.8 all-reduce.1
  653.2 153.1 reduce-scatter.2
where the time goes:
time: 816 us; the launch traced here: 815 us
  waiting for transfers between devices  725 us (89%)
  matrix products  43.5 us (5%)
  local copies, waits for them, and re-layouts  18.2 us (2%)
  between operations  14.1 us (2%)
  other arithmetic  12.3 us (2%)
    psum x1, waiting for transfers between devices, per_device(): stacked = lax.psum(stacked, 'dp')  254 us
    reduce_scatter x1, waiting for transfers between devices, per_device(): lax.psum_scatter(partial_out, 'tensor', scatter_dimension=0, tiled=True)  153 us
    reduce_scatter x1, waiting for transfers between devices, per_device(): lax.psum_scatter(lax.dot_general(all_cotangent, weight, (((1,), (1,)), ((...  139 us
    all_gather x1, waiting for transfers between devices, per_device(): all_cotangent = lax.all_gather(cotangent, 'tensor', axis=0, tiled=True)  90.3 us
    all_gather x1, waiting for transfers between devices, per_device(): lax.all_gather(rotated, 'dp', axis=0, tiled=True)  66.4 us
    ppermute x4, waiting for transfers between devices, swapped(): lax.ppermute(shard, axis, [(i, i ^ 1 << bit) for i in range(lax.axis_size...  21.6 us
  transfers between devices with their start and end apart: 9, of which 8 were waited for; matrix products, arithmetic and copies ran while one was open for 7% of the time, Pallas kernels for 0%

commit v1 on v0

v1 whole, which is shorter than its diff:
```python
import jax
import jax.numpy as jnp
from jax import lax
from jax.experimental import pallas as pl
from jax.experimental.pallas import tpu as pltpu
from jax.sharding import PartitionSpec as P

HIGH = lax.Precision.HIGHEST
F32 = jnp.float32
BF16 = jnp.bfloat16
MESH = pl.DeviceIdType.MESH


def swapped(shard, axis, bit):
    return lax.ppermute(shard, axis, [(i, i ^ 1 << bit) for i in range(lax.axis_size(axis))])


def first_backward(grad_out, inputs, coeffs, block):
    rows, width = grad_out.shape
    count = width // block
    viewed = grad_out.reshape(rows, count, block)
    grad_coeffs = jnp.einsum("tqk,tqc->kqc", inputs, viewed, precision=HIGH).reshape(block, width)
    grad_inputs = jnp.einsum(
        "tqc,kqc->tqk", viewed, coeffs.reshape(block, count, block), precision=HIGH
    )
    return (grad_out + grad_inputs.reshape(rows, width), grad_coeffs)


def second_backward(grad_out, inputs, coeffs, block):
    rows, width = grad_out.shape
    half = block // 2
    count = width // (2 * block)
    viewed = grad_out.reshape(rows, count, 2, 2, half)
    grad_coeffs = jnp.einsum("tqak,tqbaw->kqbaw", inputs, viewed, precision=HIGH).reshape(
        block, width
    )
    grad_inputs = jnp.einsum(
        "tqbaw,kqbaw->tqak", viewed, coeffs.reshape(block, count, 2, 2, half), precision=HIGH
    )
    grad_inputs = grad_inputs.reshape(rows, count, 2, 2, half).transpose(0, 1, 3, 2, 4)
    return (grad_out + grad_inputs.reshape(rows, width), grad_coeffs)


def lower_side(bit):
    return lax.axis_index("tensor") // (1 << bit) % 2 == 0


def cross_inputs(own, partner, block, bit):
    rows, width = own.shape
    half = block // 2
    mine = own.reshape(rows, width // half, half)
    theirs = partner.reshape(rows, width // half, half)
    return jnp.where(
        lower_side(bit), jnp.concatenate([mine, theirs], 2), jnp.concatenate([theirs, mine], 2)
    )


def cross_backward(grad_out, inputs, coeffs, block, bit):
    rows, width = grad_out.shape
    half = block // 2
    viewed = grad_out.reshape(rows, width // half, half)
    grad_coeffs = jnp.einsum("thk,thw->khw", inputs, viewed, precision=HIGH).reshape(block, width)
    grad_inputs = jnp.einsum(
        "thw,khw->thk", viewed, coeffs.reshape(block, width // half, half), precision=HIGH
    )
    lower = lower_side(bit)
    own_part = jnp.where(lower, grad_inputs[:, :, :half], grad_inputs[:, :, half:])
    other_part = jnp.where(lower, grad_inputs[:, :, half:], grad_inputs[:, :, :half])
    arrived = swapped(other_part.reshape(rows, width), "tensor", bit)
    return (grad_out + own_part.reshape(rows, width) + arrived, grad_coeffs)


def hdot(a, b):
    return jnp.dot(a, b, precision=HIGH, preferred_element_type=F32)


def quarter_masks():
    r = lax.broadcasted_iota(jnp.int32, (128, 128), 0) // 32
    c = lax.broadcasted_iota(jnp.int32, (128, 128), 1) // 32
    return (r // 2 == c // 2, r % 2 == c % 2, r == c)


def local_matrix(coeffs, masks, section):
    if section == 0:
        stacked = jnp.concatenate([coeffs, coeffs], 0)
    else:
        stacked = jnp.concatenate([coeffs[:32], coeffs[:32], coeffs[32:], coeffs[32:]], 0)
    return jnp.where(masks[section], stacked, 0.0)


def cross_matrices(coeffs, masks, lower):
    first, second = coeffs[:32], coeffs[32:]
    own = jnp.where(lower, first, second)
    other = jnp.where(lower, second, first)
    return [jnp.where(masks[2], jnp.concatenate([part] * 4, 0), 0.0) for part in (own, other)]


def local_section(src, dst, factors, masks, section):
    for q in range(6):
        cols = pl.ds(128 * q, 128)
        field = src[:, cols].astype(F32)
        dst[:, cols] = field + hdot(field, local_matrix(factors[section, :, cols], masks, section))


def cross_section(src, partner, put, factors, masks, section, lower):
    for q in range(6):
        cols = pl.ds(128 * q, 128)
        own, other = cross_matrices(factors[section, :, cols], masks, lower)
        field = src[:, cols]
        put(cols, field + hdot(field, own) + hdot(partner[:, cols].astype(F32), other))


def main_kernel(
    tokens, w_own, factors, w_hbm, cot_hbm,
    proj, z1, z2, p2, z3, p3, g4,
    zsend, rot, R, cotG, w_oth, bsib, bsib_in, bown, up_out, up_in, dn_out, dn_in,
    pbuf, px_out, px_in, gsend, gin,
    loc_sem, sx, rx, sy, ry, sc, rc, sw, rw, sys, yr, sR, rR, sS, rS, sB, rB, sZ, rZ, sP, rP,
    sG, rG,
):
    dp, tn = lax.axis_index("dp"), lax.axis_index("tensor")
    core, z, yh = dp % 2, dp // 2 % 8, dp // 16
    x, yl = tn % 4, tn // 4

    def dev(yh=yh, z=z, core=core, yl=yl, x=x):
        return (yh * 16 + z * 2 + core, yl * 4 + x)

    right, left = dev(x=(x + 1) % 4), dev(x=(x + 3) % 4)
    xpair = dev(x=x + 1 - 2 * (x % 2))
    ypair = dev(yl=1 - yl)
    sibling = dev(core=1 - core)
    above, below = dev(z=(z + 1) % 8), dev(z=(z + 7) % 8)
    diagonal = yh == yl

    sent = []

    def rcopy(src, dst, ssem, rsem, to):
        return pltpu.make_async_remote_copy(
            src_ref=src, dst_ref=dst, send_sem=ssem, recv_sem=rsem,
            device_id=to, device_id_type=MESH,
        )

    def send(src, dst, ssem, rsem, to):
        copy = rcopy(src, dst, ssem, rsem, to)
        copy.start()
        sent.append(copy)

    def arrived(dst, rsem):
        rcopy(dst, dst, rsem, rsem, sibling).wait_recv()

    barrier = pltpu.get_barrier_semaphore()
    for peer in (right, left, ypair, sibling, above, below):
        pl.semaphore_signal(barrier, inc=1, device_id=peer, device_id_type=MESH)
    for peer, here in (
        (dev(yh=0, yl=yh), (yh == 0) & diagonal),
        (dev(yh=1, yl=yh), (yh == 1) & diagonal),
        (dev(yh=yl, yl=0), (yl == 0) & diagonal),
        (dev(yh=yl, yl=1), (yl == 1) & diagonal),
    ):
        @pl.when(jnp.logical_not(here))
        def _():
            pl.semaphore_signal(barrier, inc=1, device_id=peer, device_id_type=MESH)
    pl.semaphore_wait(barrier, 10 - 2 * diagonal.astype(jnp.int32))

    def half(index):
        return cotG.at[index]

    own_cot = [pltpu.make_async_copy(cot_hbm.at[pl.ds(256 * i, 256)], half(2 * x + i), loc_sem.at[i]) for i in range(2)]
    for copy in own_cot:
        copy.start()

    masks = quarter_masks()
    local_section(tokens, z1, factors, masks, 0)
    local_section(z1, z2, factors, masks, 1)
    zsend[0] = z2[...].astype(BF16)
    send(zsend.at[0], zsend.at[2], sx.at[0], rx.at[0], xpair)

    for i, to in ((0, right), (1, left), (1, right), (0, left)):
        n = i + (0 if to is right else 2)
        send(cot_hbm.at[pl.ds(256 * i, 256)], half(2 * x + i), sc.at[n], rc.at[n], to)

    def send_w(i):
        rows = pl.ds(256 * i, 256)
        send(w_hbm.at[rows], w_oth.at[rows], sw.at[i], rw.at[i], ypair)

    send_w(0)
    arrived(zsend.at[2], rx.at[0])
    p2[...] = zsend[2].astype(F32)

    def put3(cols, value):
        z3[:, cols] = value
        zsend[1, :, cols] = value.astype(BF16)

    cross_section(z2, p2, put3, factors, masks, 2, x % 2 == 0)
    send(zsend.at[1], zsend.at[3], sy.at[0], ry.at[0], ypair)
    arrived(zsend.at[3], ry.at[0])
    p3[...] = zsend[3].astype(F32)

    def put4(cols, value):
        rot[:, cols] = value.astype(BF16)

    cross_section(z3, p3, put4, factors, masks, 3, yl == 0)

    slot = (yl + yh) % 2
    for b in range(2):
        copy = rcopy(rot, R.at[z, slot, core], sys.at[b], yr.at[slot], dev(yh=b, yl=yh))
        pl.when(jnp.logical_not((yh == b) & diagonal))(copy.start)

    @pl.when(diagonal)
    def _():
        R[z, 0, core] = rot[...]

    send_w(1)
    send_w(2)

    def spread(zz, s, up, down, k):
        block = R.at[zz, s, core]
        if up:
            send(block, block, sR.at[0, k, s], rR.at[0, k, s], above)
        if down:
            send(block, block, sR.at[1, k, s], rR.at[1, k, s], below)
        send(block, block, sS.at[zz, s], rS.at[zz, s], sibling)

    @pl.when(jnp.logical_not(diagonal))
    def _():
        arrived(R.at[z, 0, core], yr.at[0])
    spread(z, 0, True, True, 0)
    arrived(R.at[z, 1, core], yr.at[1])
    spread(z, 1, True, True, 0)

    def step(k):
        lo, hi = (z + 8 - k) % 8, (z + k) % 8
        for s in range(2):
            arrived(R.at[lo, s, core], rR.at[0, k - 1, s])
            spread(lo, s, k < 3 or s == 0, False, k)
            arrived(R.at[hi, s, core], rR.at[1, k - 1, s])
            spread(hi, s, False, k < 3 or s == 1, k)

    step(1)
    xl, xr = (x + 3) % 4, (x + 1) % 4
    arrived(half(2 * xl), rc.at[0])
    send(half(2 * xl), half(2 * xl), sc.at[4], rc.at[4], right)
    arrived(half(2 * xr + 1), rc.at[3])
    send(half(2 * xr + 1), half(2 * xr + 1), sc.at[5], rc.at[5], left)
    step(2)
    step(3)

    xo = (x + 2) % 4
    arrived(half(2 * xl + 1), rc.at[1])
    arrived(half(2 * xr), rc.at[2])
    arrived(half(2 * xo), rc.at[4])
    arrived(half(2 * xo + 1), rc.at[5])
    for copy in own_cot:
        copy.wait()
    for i in range(3):
        arrived(w_oth.at[pl.ds(256 * i, 256)], rw.at[i])

    def back_block(n, carry):
        zz = (z + 4 + n) % 8
        left_side = cotG[zz]
        for s, w in ((0, w_own), (1, w_oth)):
            part = lax.dot_general(left_side, w[...], (((1,), (1,)), ((), ())), preferred_element_type=F32)

            @pl.when(core == 0)
            def _():
                bown[zz, s] = part[:128]
                bsib[zz, s] = part[128:].astype(BF16)

            @pl.when(core == 1)
            def _():
                bown[zz, s] = part[128:]
                bsib[zz, s] = part[:128].astype(BF16)
        rcopy(bsib.at[zz], bsib_in.at[zz], sB.at[zz], rB.at[zz], sibling).start()
        return carry

    lax.fori_loop(0, 8, back_block, 0)

    zf = (z + 4) % 8
    arrived(R.at[zf, 0, core], rR.at[0, 3, 0])
    spread(zf, 0, False, False, 4)
    arrived(R.at[zf, 1, core], rR.at[1, 3, 1])
    spread(zf, 1, False, False, 4)

    def own_back(zz, s):
        return bown[zz, s] + bsib_in[zz, s].astype(F32)

    def back_ready(zz):
        arrived(bsib_in.at[zz], rB.at[zz])

    def ring_send(direction, n, zz, s, incoming):
        out, into = (up_out, up_in) if direction == 0 else (dn_out, dn_in)
        value = own_back(zz, s)
        if incoming is not None:
            arrived(into.at[incoming], rZ.at[direction, incoming])
            value = value + into[incoming].astype(F32)
        out[n] = value.astype(BF16)
        send(out.at[n], into.at[n], sZ.at[direction, n], rZ.at[direction, n], above if direction == 0 else below)

    def z_at(k):
        return (z + 8 + k) % 8

    back_ready(z_at(4))
    ring_send(0, 0, z_at(4), 0, None)
    ring_send(1, 0, z_at(4), 1, None)
    back_ready(z_at(3))
    back_ready(z_at(-3))
    ring_send(0, 1, z_at(3), 1, None)
    ring_send(1, 1, z_at(-3), 0, None)

    for n in range(8):
        for s in range(2):
            block = R.at[n, s, 1 - core]
            arrived(block, rS.at[n, s])

    def product(zz):
        return jnp.dot(R[zz, 0].reshape(256, 768), w_own[...], preferred_element_type=F32) + jnp.dot(
            R[zz, 1].reshape(256, 768), w_oth[...], preferred_element_type=F32
        )

    def px_send(direction, n, zz, incoming):
        value = product(zz)
        if incoming is not None:
            arrived(px_in.at[direction, incoming], rP.at[direction, incoming])
            value = value + px_in[direction, incoming].astype(F32)
        px_out[direction, n] = value.astype(BF16)
        send(px_out.at[direction, n], px_in.at[direction, n], sP.at[direction, n], rP.at[direction, n], right if direction == 0 else left)

    px_send(0, 0, 2 * xo, None)
    px_send(1, 0, 2 * xo + 1, None)
    ring_send(0, 2, z_at(3), 0, 0)
    ring_send(1, 2, z_at(-3), 1, 0)
    px_send(0, 1, 2 * xr + 1, None)
    px_send(1, 1, 2 * xl, None)
    back_ready(z_at(2))
    back_ready(z_at(-2))
    ring_send(0, 3, z_at(2), 1, 1)
    ring_send(1, 3, z_at(-2), 0, 1)
    ring_send(0, 4, z_at(2), 0, 2)
    ring_send(1, 4, z_at(-2), 1, 2)
    px_send(0, 2, 2 * xr, 0)
    px_send(1, 2, 2 * xl + 1, 0)
    back_ready(z_at(1))
    back_ready(z_at(-1))
    ring_send(0, 5, z_at(1), 1, 3)
    ring_send(1, 5, z_at(-1), 0, 3)
    ring_send(0, 6, z_at(1), 0, 4)
    ring_send(1, 6, z_at(-1), 1, 4)
    back_ready(z)
    pbuf[0] = product(2 * x)
    pbuf[1] = product(2 * x + 1)

    for s, nu, nd in ((1, 5, 6), (0, 6, 5)):
        arrived(up_in.at[nu], rZ.at[0, nu])
        arrived(dn_in.at[nd], rZ.at[1, nd])
        gsend[s] = (own_back(z, s) + up_in[nu].astype(F32) + dn_in[nd].astype(F32)).astype(BF16)
        copy = rcopy(gsend.at[s], gin.at[yh], sG.at[s], rG.at[yh], dev(yh=yl, yl=(yl + s) % 2))
        if s == 1:
            copy.start()
        else:
            pl.when(jnp.logical_not(diagonal))(copy.start)

    @pl.when(diagonal)
    def _():
        gin[yh] = gsend[0]

    for a in range(2):
        @pl.when(jnp.logical_not((yh == a) & diagonal))
        def _():
            arrived(gin.at[a], rG.at[a])
    g4[...] = gin[0].astype(F32) + gin[1].astype(F32)

    arrived(px_in.at[0, 2], rP.at[0, 2])
    arrived(px_in.at[1, 1], rP.at[1, 1])
    proj[pl.ds(0, 256), :] = (pbuf[0] + px_in[0, 2].astype(F32) + px_in[1, 1].astype(F32)).astype(BF16)
    arrived(px_in.at[0, 1], rP.at[0, 1])
    arrived(px_in.at[1, 2], rP.at[1, 2])
    proj[pl.ds(256, 256), :] = (pbuf[1] + px_in[0, 1].astype(F32) + px_in[1, 2].astype(F32)).astype(BF16)

    for copy in sent:
        copy.wait_send()
    for b in range(2):
        copy = rcopy(rot, R.at[z, slot, core], sys.at[b], yr.at[slot], dev(yh=b, yl=yh))
        pl.when(jnp.logical_not((yh == b) & diagonal))(copy.wait_send)
    for n in range(8):
        rcopy(bsib.at[n], bsib_in.at[n], sB.at[n], rB.at[n], sibling).wait_send()
    rcopy(gsend.at[1], gin.at[0], sG.at[1], rG.at[0], ypair).wait_send()
    pl.when(jnp.logical_not(diagonal))(rcopy(gsend.at[0], gin.at[0], sG.at[0], rG.at[0], ypair).wait_send)


def main_call(tokens, weight, factors, cotangent):
    V = pltpu.VMEM
    D = pltpu.SemaphoreType.DMA
    field = jax.ShapeDtypeStruct((128, 768), F32)
    vm = pl.BlockSpec(memory_space=pltpu.VMEM)
    hbm = pl.BlockSpec(memory_space=pl.ANY)
    return pl.pallas_call(
        main_kernel,
        out_shape=(jax.ShapeDtypeStruct((512, 896), BF16),) + (field,) * 6,
        in_specs=[vm, vm, vm, hbm, hbm],
        out_specs=(vm,) * 7,
        scratch_shapes=[
            V((4, 128, 768), BF16),
            V((128, 768), BF16),
            V((8, 2, 2, 128, 768), BF16),
            V((8, 256, 896), BF16),
            V((768, 896), BF16),
            V((8, 2, 128, 768), BF16),
            V((8, 2, 128, 768), BF16),
            V((8, 2, 128, 768), F32),
            V((7, 128, 768), BF16),
            V((7, 128, 768), BF16),
            V((7, 128, 768), BF16),
            V((7, 128, 768), BF16),
            V((2, 256, 896), F32),
            V((2, 3, 256, 896), BF16),
            V((2, 3, 256, 896), BF16),
            V((2, 128, 768), BF16),
            V((2, 128, 768), BF16),
            D((2,)),
            D((1,)), D((1,)), D((1,)), D((1,)),
            D((6,)), D((6,)), D((3,)), D((3,)),
            D((2,)), D((2,)),
            D((2, 4, 2)), D((2, 4, 2)),
            D((8, 2)), D((8, 2)),
            D((8,)), D((8,)),
            D((2, 7)), D((2, 7)),
            D((2, 3)), D((2, 3)),
            D((2,)), D((2,)),
        ],
        compiler_params=pltpu.CompilerParams(
            collective_id=0, has_side_effects=True, vmem_limit_bytes=56 * 1024 * 1024
        ),
        name="rotate_project",
    )(tokens, weight, factors, weight, cotangent)


def per_device(tokens, weight, factors, cotangent):
    block = factors.shape[1]
    top_bit = lax.axis_size("tensor").bit_length() - 2
    projected, z1, z2, p2, z3, p3, back = main_call(tokens, weight, factors, cotangent)
    rows, width = tokens.shape
    inputs0 = tokens.astype(F32).reshape(rows, width // block, block)
    inputs1 = z1.reshape(rows, width // (2 * block), 2, 2, block // 2).transpose(0, 1, 3, 2, 4)
    inputs1 = inputs1.reshape(rows, width // (2 * block), 2, block)
    inputs2 = cross_inputs(z2, p2, block, 0)
    inputs3 = cross_inputs(z3, p3, block, top_bit)
    grad_now, grad_three = cross_backward(back, inputs3, factors[3], block, top_bit)
    grad_now, grad_two = cross_backward(grad_now, inputs2, factors[2], block, 0)
    grad_now, grad_one = second_backward(grad_now, inputs1, factors[1], block)
    grad_now, grad_zero = first_backward(grad_now, inputs0, factors[0], block)
    stacked = jnp.stack([grad_zero, grad_one, grad_two, grad_three])
    stacked = lax.psum(stacked, "dp")
    return (projected, grad_now, stacked)


def solution(mesh):
    placed = (P("dp", "tensor"), P("tensor", "dp"), P(None, None, "tensor"), P("tensor", "dp"))
    return jax.shard_map(
        per_device,
        mesh=mesh,
        in_specs=placed,
        out_specs=(P("tensor", "dp"), P("dp", "tensor"), P(None, None, "tensor")),
        check_vma=False,
    )
```

time: 816 us -> 433 us (0.53)
  waiting for transfers between devices: 725 us -> 272 us
  Pallas kernels: 0 us -> 114 us
  matrix products: 43.5 us -> 11.4 us
    reduce_scatter x2 -> x0, waiting for transfers between devices: 292 us -> none  [the longest x1 153 us: per_device(): lax.psum_scatter(partial_out, 'tensor', scatter_dimension=0, tiled=True)]
    all_gather x2 -> x0, waiting for transfers between devices: 157 us -> none  [the longest x1 90.3 us: per_device(): all_cotangent = lax.all_gather(cotangent, 'tensor', axis=0, tiled=True)]
    pallas_call x0 -> x1, Pallas kernels: none -> 114 us  [main_call(): pl.pallas_call(main_kernel, out_shape=(jax.ShapeDtypeStruct((512, 896), B...]
    dot_general x6 -> x0, matrix products: 29.9 us -> none  [the longest x1 12.4 us: per_device(): jnp.dot(lax.all_gather(rotated, 'dp', axis=0, tiled=True), weight, prefer...]
    ppermute x4 -> x2, waiting for transfers between devices: 21.6 us -> 3.48 us  [swapped(): lax.ppermute(shard, axis, [(i, i ^ 1 << bit) for i in range(lax.axis_size...]
    psum x1, waiting for transfers between devices: 254 us -> 268 us  [per_device(): stacked = lax.psum(stacked, 'dp')]
  transfers between devices with their start and end apart: 9 -> 3, of which waited for: 8 -> 3; matrix products, arithmetic and copies ran while one was open for 7% -> 3% of each run, Pallas kernels for 0% -> 0%
where the time goes in v1:
time: 433 us; the launch traced here: 432 us
  waiting for transfers between devices  272 us (63%)
  Pallas kernels  114 us (26%)
  local copies, waits for them, and re-layouts  16.6 us (4%)
  between operations  14.3 us (3%)
  matrix products  11.4 us (3%)
    psum x1, waiting for transfers between devices, per_device(): stacked = lax.psum(stacked, 'dp')  268 us
    pallas_call x1, Pallas kernels, main_call(): pl.pallas_call(main_kernel, out_shape=(jax.ShapeDtypeStruct((512, 896), B...  114 us
  transfers between devices with their start and end apart: 3, of which 3 were waited for; matrix products, arithmetic and copies ran while one was open for 3% of the time, Pallas kernels for 0%

profile of v1, /device:TPU:1, one launch (start us, length us, event | category | flops | bytes accessed | tf_op | source)
XLA Modules:
  0.0 432.2 jit_solution(3364238120540758699)
XLA Ops:
  7.2 1.3 fusion.22
  8.5 113.6 %rotate_project.1 = (bf16[512,896]{1,0:T(8,128)(2,1)}, f32[128,768]{1,0:T(8,128)}, f32[128,768]{1,0:T(8,128)}, f32[128,768]{1,0:T(8,128)}, f32[128,768]{1,0:T(8,...) custom-call(bf16[128,768]{1,0:T(8,128)(2,1)} %tokens.1, bf16[768,896]{1,0:T(8,128)(2,1)} %w_hbm.1, f32[4,64,768]{2,1,0:T(8,128)} %factors.1, ...), custom_call_target="tpu_custom_call" | custom-call | tf_op jit(solution)/shard_map/rotate_project/pallas_call | solution.py:396
  122.2 1.2 copy.62
  123.5 1.4 convolution_bitcast_fusion.1
  125.0 0.9 copy.65
  127.1 0.9 copy.84
  128.0 2.0 copy.85
  130.2 1.9 copy.86
  132.1 0.9 copy.87
  133.0 1.7 collective-permute-done
  134.7 1.1 add_add_fusion.1
  136.0 1.4 convolution_bitcast_fusion
  137.5 0.9 copy.69
  138.4 3.5 fusion.6
  142.0 2.5 fusion
  144.5 1.7 collective-permute-done.1
  146.3 1.1 add_add_fusion
  147.5 0.7 convolution_bitcast_fusion.2
  148.3 0.8 fusion.14
  150.3 1.2 pad_maximum_fusion
  152.4 0.8 add.38
  153.2 268.5 %all-reduce.2.cloned.1.call-done = f32[4,64,768]{1,2,0:T(8,128)} async-done(((f32[4,64,768]{1,2,0:T(8,128)}), f32[4,64,768]{1,2,0:T(8,128)}) %all-reduce.2.cloned.1.call-update) | async-done | bytes 786448 | tf_op jit(solution)/shard_map/psum | solution.py:452
  421.7 2.7 copy.88
  424.5 0.9 copy.102
  (41 shorter events, 4.2 us)
Async XLA Ops:
  7.2 414.6 %all-reduce.2.cloned.1.call-start = ((), (), s32[]{:S(2)}) async-start(), calls=%async_computation | async-start | bytes 3145728 | tf_op jit(solution)/shard_map/psum | solution.py:452
  124.9 1.0 copy-start.2
  125.0 1.5 copy-start.6
  125.9 8.8 %collective-permute-start = (f32[128,768]{1,0:T(8,128)}, f32[128,768]{1,0:T(8,128)}, u32[]{:S(2)}, u32[]{:S(2)}) collective-permute-start(f32[128,768]{1,0:T(8,128)} %copy.65), channel_id=1, source_target_pairs={{0,4},{1,5},{2,6},{3,7},{4,0},{5,1},{6,2},{7,3},{8,12},{9,13},{10,... | collective-permute-start | bytes 1179656 | tf_op jit(solution)/shard_map/ppermute | solution.py:15
  126.1 1.0 copy-start.5
  126.7 5.4 %copy-start.4 = (f32[128,768]{1,0:T(8,128)S(1)}, f32[128,768]{1,0:T(8,128)}, u32[]{:S(2)}) copy-start(f32[128,768]{1,0:T(8,128)} %get-tuple-element.16) | copy-start | bytes 1179652
  128.0 6.7 %copy-start = (f32[128,768]{1,0:T(8,128)S(1)}, f32[128,768]{1,0:T(8,128)}, u32[]{:S(2)}) copy-start(f32[128,768]{1,0:T(8,128)} %get-tuple-element.11) | copy-start | bytes 1179652
  138.4 3.7 copy-start.7
  138.4 7.9 %collective-permute-start.1 = (f32[128,768]{1,0:T(8,128)}, f32[128,768]{1,0:T(8,128)}, u32[]{:S(2)}, u32[]{:S(2)}) collective-permute-start(f32[128,768]{1,0:T(8,128)} %copy.69), channel_id=1, source_target_pairs={{0,1},{1,0},{2,3},{3,2},{4,5},{5,4},{6,7},{7,6},{8,9},{9,8},{10,11... | collective-permute-start | bytes 1179656 | tf_op jit(solution)/shard_map/ppermute | solution.py:15
  149.3 1.0 copy-start.3
  152.4 272.0 %copy-start.1 = (bf16[512,896]{1,0:T(8,128)(2,1)S(1)}, bf16[512,896]{1,0:T(8,128)(2,1)}, u32[]{:S(2)}) copy-start(bf16[512,896]{1,0:T(8,128)(2,1)} %get-tuple-element.34) | copy-start | bytes 2752516
Sparse Core Ops, SparseCore 0:
  151.6 270.0 all-reduce.1

commit v2 on v1

--- a/solution.py
+++ b/solution.py
@@ -11,67 +11,16 @@
 MESH = pl.DeviceIdType.MESH
 
 
-def swapped(shard, axis, bit):
-    return lax.ppermute(shard, axis, [(i, i ^ 1 << bit) for i in range(lax.axis_size(axis))])
-
-
-def first_backward(grad_out, inputs, coeffs, block):
-    rows, width = grad_out.shape
-    count = width // block
-    viewed = grad_out.reshape(rows, count, block)
-    grad_coeffs = jnp.einsum("tqk,tqc->kqc", inputs, viewed, precision=HIGH).reshape(block, width)
-    grad_inputs = jnp.einsum(
-        "tqc,kqc->tqk", viewed, coeffs.reshape(block, count, block), precision=HIGH
-    )
-    return (grad_out + grad_inputs.reshape(rows, width), grad_coeffs)
-
-
-def second_backward(grad_out, inputs, coeffs, block):
-    rows, width = grad_out.shape
-    half = block // 2
-    count = width // (2 * block)
-    viewed = grad_out.reshape(rows, count, 2, 2, half)
-    grad_coeffs = jnp.einsum("tqak,tqbaw->kqbaw", inputs, viewed, precision=HIGH).reshape(
-        block, width
-    )
-    grad_inputs = jnp.einsum(
-        "tqbaw,kqbaw->tqak", viewed, coeffs.reshape(block, count, 2, 2, half), precision=HIGH
-    )
-    grad_inputs = grad_inputs.reshape(rows, count, 2, 2, half).transpose(0, 1, 3, 2, 4)
-    return (grad_out + grad_inputs.reshape(rows, width), grad_coeffs)
-
-
-def lower_side(bit):
-    return lax.axis_index("tensor") // (1 << bit) % 2 == 0
-
-
-def cross_inputs(own, partner, block, bit):
-    rows, width = own.shape
-    half = block // 2
-    mine = own.reshape(rows, width // half, half)
-    theirs = partner.reshape(rows, width // half, half)
-    return jnp.where(
-        lower_side(bit), jnp.concatenate([mine, theirs], 2), jnp.concatenate([theirs, mine], 2)
-    )
-
-
-def cross_backward(grad_out, inputs, coeffs, block, bit):
-    rows, width = grad_out.shape
-    half = block // 2
-    viewed = grad_out.reshape(rows, width // half, half)
-    grad_coeffs = jnp.einsum("thk,thw->khw", inputs, viewed, precision=HIGH).reshape(block, width)
-    grad_inputs = jnp.einsum(
-        "thw,khw->thk", viewed, coeffs.reshape(block, width // half, half), precision=HIGH
-    )
-    lower = lower_side(bit)
-    own_part = jnp.where(lower, grad_inputs[:, :, :half], grad_inputs[:, :, half:])
-    other_part = jnp.where(lower, grad_inputs[:, :, half:], grad_inputs[:, :, :half])
-    arrived = swapped(other_part.reshape(rows, width), "tensor", bit)
-    return (grad_out + own_part.reshape(rows, width) + arrived, grad_coeffs)
-
-
 def hdot(a, b):
     return jnp.dot(a, b, precision=HIGH, preferred_element_type=F32)
+
+
+def hdot_nt(a, b):
+    return lax.dot_general(a, b, (((1,), (1,)), ((), ())), precision=HIGH, preferred_element_type=F32)
+
+
+def hdot_tn(a, b):
+    return lax.dot_general(a, b, (((0,), (0,)), ((), ())), precision=HIGH, preferred_element_type=F32)
 
 
 def quarter_masks():
@@ -110,13 +59,19 @@
         put(cols, field + hdot(field, own) + hdot(partner[:, cols].astype(F32), other))
 
 
+def fold_cross(full, masks):
+    full = jnp.where(masks[2], full, 0.0)
+    return full[:32] + full[32:64] + full[64:96] + full[96:]
+
+
 def main_kernel(
     tokens, w_own, factors, w_hbm, cot_hbm,
-    proj, z1, z2, p2, z3, p3, g4,
+    proj, grad_tokens, grad_factors,
+    z1, z2, p2, z3, p3, ga, gb, gf, cin, gh, ain, res, fout,
     zsend, rot, R, cotG, w_oth, bsib, bsib_in, bown, up_out, up_in, dn_out, dn_in,
     pbuf, px_out, px_in, gsend, gin,
     loc_sem, sx, rx, sy, ry, sc, rc, sw, rw, sys, yr, sR, rR, sS, rS, sB, rB, sZ, rZ, sP, rP,
-    sG, rG,
+    sG, rG, sC, rC, sA, rA, sF, rF, sH, rH,
 ):
     dp, tn = lax.axis_index("dp"), lax.axis_index("tensor")
     core, z, yh = dp % 2, dp // 2 % 8, dp // 16
@@ -149,8 +104,18 @@
         rcopy(dst, dst, rsem, rsem, sibling).wait_recv()
 
     barrier = pltpu.get_barrier_semaphore()
-    for peer in (right, left, ypair, sibling, above, below):
+    for peer in (right, left, ypair, sibling):
         pl.semaphore_signal(barrier, inc=1, device_id=peer, device_id_type=MESH)
+    chip = yh * 8 + z
+
+    def chip_dev(index):
+        return dev(yh=index // 8, z=index % 8)
+
+    def greet(r, carry):
+        pl.semaphore_signal(barrier, inc=1, device_id=chip_dev((chip + r) % 16), device_id_type=MESH)
+        return carry
+
+    lax.fori_loop(1, 16, greet, 0)
     for peer, here in (
         (dev(yh=0, yl=yh), (yh == 0) & diagonal),
         (dev(yh=1, yl=yh), (yh == 1) & diagonal),
@@ -160,7 +125,7 @@
         @pl.when(jnp.logical_not(here))
         def _():
             pl.semaphore_signal(barrier, inc=1, device_id=peer, device_id_type=MESH)
-    pl.semaphore_wait(barrier, 10 - 2 * diagonal.astype(jnp.int32))
+    pl.semaphore_wait(barrier, 23 - 2 * diagonal.astype(jnp.int32))
 
     def half(index):
         return cotG.at[index]
@@ -367,14 +332,107 @@
         @pl.when(jnp.logical_not((yh == a) & diagonal))
         def _():
             arrived(gin.at[a], rG.at[a])
-    g4[...] = gin[0].astype(F32) + gin[1].astype(F32)
-
+    ga[...] = gin[0].astype(F32) + gin[1].astype(F32)
+
+    def reduce_start(s):
+        send(gf.at[s, pl.ds(32 * (1 - core), 32)], cin.at[s], sC.at[s], rC.at[s], sibling)
+
+    def owner_slot(s, j):
+        owner = 8 * (s // 2) + 2 * j + s % 2
+        r = (chip + 16 - owner) % 16
+        copy = rcopy(gh.at[s, pl.ds(8 * j, 8)], ain.at[r], sA.at[s, j], rA.at[r], chip_dev(owner))
+        return r, copy
+
+    def reduce_middle(s):
+        arrived(cin.at[s], rC.at[s])
+        gh[s] = gf[s, pl.ds(32 * core, 32), :] + cin[s]
+        for j in range(4):
+            r, copy = owner_slot(s, j)
+            pl.when(r != 0)(copy.start)
+
+    own_s, own_rows = 2 * yh + z % 2, pl.ds(8 * (z // 2), 8)
+
+    def peer_copy(r):
+        place = fout.at[core, own_s, own_rows]
+        return rcopy(res, place, sF.at[r], rF.at[chip], chip_dev((chip + r) % 16))
+
+    def own_work():
+        def add(r, total):
+            arrived(ain.at[r], rA.at[r])
+            return total + ain[r]
+
+        total = lax.fori_loop(1, 16, add, gh[own_s, own_rows, :])
+        res[...] = total
+        fout[core, own_s, own_rows, :] = total
+
+        def push(r, carry):
+            peer_copy(r).start()
+            return carry
+
+        lax.fori_loop(1, 16, push, 0)
+
+    def cross_back(g, out, section, saved, partner, bit, peer, ssem, rsem, a, b):
+        lower = bit == 0
+        kept = []
+        for q in range(6):
+            cols = pl.ds(128 * q, 128)
+            own, other = cross_matrices(factors[section, :, cols], masks, lower)
+            zsend[a, :, cols] = hdot_nt(g[:, cols], other).astype(BF16)
+            kept.append(own)
+        send(zsend.at[a], zsend.at[b], ssem, rsem, peer)
+        for q in range(6):
+            cols = pl.ds(128 * q, 128)
+            field = g[:, cols]
+            out[:, cols] = field + hdot_nt(field, kept[q])
+            gf[section, pl.ds(32 * bit, 32), cols] = fold_cross(hdot_tn(saved[:, cols], field), masks)
+            gf[section, pl.ds(32 * (1 - bit), 32), cols] = fold_cross(hdot_tn(partner[:, cols], field), masks)
+        reduce_start(section)
+        arrived(zsend.at[b], rsem)
+        out[...] += zsend[b].astype(F32)
+
+    def local_back(g, out, section, saved):
+        for q in range(6):
+            cols = pl.ds(128 * q, 128)
+            field = g[:, cols]
+            out[:, cols] = field + hdot_nt(field, local_matrix(factors[section, :, cols], masks, section))
+        for q in range(6):
+            cols = pl.ds(128 * q, 128)
+            full = jnp.where(masks[section], hdot_tn(saved[:, cols].astype(F32), g[:, cols]), 0.0)
+            if section == 0:
+                gf[0, :, cols] = full[:64] + full[64:]
+            else:
+                gf[1, pl.ds(0, 32), cols] = full[:32] + full[32:64]
+                gf[1, pl.ds(32, 32), cols] = full[64:96] + full[96:]
+        reduce_start(section)
+
+    cross_back(ga, gb, 3, z3, p3, yl, ypair, sy.at[1], ry.at[1], 4, 5)
+    cross_back(gb, ga, 2, z2, p2, x % 2, xpair, sx.at[1], rx.at[1], 6, 7)
+    reduce_middle(3)
+    reduce_middle(2)
+    local_back(ga, gb, 1, z1)
+    local_back(gb, grad_tokens, 0, tokens)
+    reduce_middle(1)
+    reduce_middle(0)
+    own_work()
     arrived(px_in.at[0, 2], rP.at[0, 2])
     arrived(px_in.at[1, 1], rP.at[1, 1])
     proj[pl.ds(0, 256), :] = (pbuf[0] + px_in[0, 2].astype(F32) + px_in[1, 1].astype(F32)).astype(BF16)
     arrived(px_in.at[0, 1], rP.at[0, 1])
     arrived(px_in.at[1, 2], rP.at[1, 2])
     proj[pl.ds(256, 256), :] = (pbuf[1] + px_in[0, 1].astype(F32) + px_in[1, 2].astype(F32)).astype(BF16)
+
+    for s in (3, 2, 1, 0):
+        for j in range(4):
+            owner = 8 * (s // 2) + 2 * j + s % 2
+
+            @pl.when(chip != owner)
+            def _():
+                arrived(fout.at[core, s, pl.ds(8 * j, 8)], rF.at[owner])
+        send(fout.at[core, s], fout.at[core, s], sH.at[s], rH.at[s], sibling)
+    for s in range(4):
+        arrived(fout.at[1 - core, s], rH.at[s])
+        grad_factors[s, pl.ds(0, 32), :] = fout[0, s]
+        grad_factors[s, pl.ds(32, 32), :] = fout[1, s]
 
     for copy in sent:
         copy.wait_send()
@@ -386,8 +444,19 @@
     rcopy(gsend.at[1], gin.at[0], sG.at[1], rG.at[0], ypair).wait_send()
     pl.when(jnp.logical_not(diagonal))(rcopy(gsend.at[0], gin.at[0], sG.at[0], rG.at[0], ypair).wait_send)
 
-
-def main_call(tokens, weight, factors, cotangent):
+    for s in range(4):
+        for j in range(4):
+            r, copy = owner_slot(s, j)
+            pl.when(r != 0)(copy.wait_send)
+
+    def drain(r, carry):
+        peer_copy(r).wait_send()
+        return carry
+
+    lax.fori_loop(1, 16, drain, 0)
+
+
+def per_device(tokens, weight, factors, cotangent):
     V = pltpu.VMEM
     D = pltpu.SemaphoreType.DMA
     field = jax.ShapeDtypeStruct((128, 768), F32)
@@ -395,11 +464,18 @@
     hbm = pl.BlockSpec(memory_space=pl.ANY)
     return pl.pallas_call(
         main_kernel,
-        out_shape=(jax.ShapeDtypeStruct((512, 896), BF16),) + (field,) * 6,
+        out_shape=(jax.ShapeDtypeStruct((512, 896), BF16), field, jax.ShapeDtypeStruct((4, 64, 768), F32)),
         in_specs=[vm, vm, vm, hbm, hbm],
-        out_specs=(vm,) * 7,
+        out_specs=(vm,) * 3,
         scratch_shapes=[
-            V((4, 128, 768), BF16),
+            *[V((128, 768), F32)] * 7,
+            V((4, 64, 768), F32),
+            V((4, 32, 768), F32),
+            V((4, 32, 768), F32),
+            V((16, 8, 768), F32),
+            V((8, 768), F32),
+            V((2, 4, 32, 768), F32),
+            V((8, 128, 768), BF16),
             V((128, 768), BF16),
             V((8, 2, 2, 128, 768), BF16),
             V((8, 256, 896), BF16),
@@ -417,7 +493,7 @@
             V((2, 128, 768), BF16),
             V((2, 128, 768), BF16),
             D((2,)),
-            D((1,)), D((1,)), D((1,)), D((1,)),
+            D((2,)), D((2,)), D((2,)), D((2,)),
             D((6,)), D((6,)), D((3,)), D((3,)),
             D((2,)), D((2,)),
             D((2, 4, 2)), D((2, 4, 2)),
@@ -426,31 +502,16 @@
             D((2, 7)), D((2, 7)),
             D((2, 3)), D((2, 3)),
             D((2,)), D((2,)),
+            D((4,)), D((4,)),
+            D((4, 4)), D((16,)),
+            D((16,)), D((16,)),
+            D((4,)), D((4,)),
         ],
         compiler_params=pltpu.CompilerParams(
             collective_id=0, has_side_effects=True, vmem_limit_bytes=56 * 1024 * 1024
         ),
         name="rotate_project",
     )(tokens, weight, factors, weight, cotangent)
-
-
-def per_device(tokens, weight, factors, cotangent):
-    block = factors.shape[1]
-    top_bit = lax.axis_size("tensor").bit_length() - 2
-    projected, z1, z2, p2, z3, p3, back = main_call(tokens, weight, factors, cotangent)
-    rows, width = tokens.shape
-    inputs0 = tokens.astype(F32).reshape(rows, width // block, block)
-    inputs1 = z1.reshape(rows, width // (2 * block), 2, 2, block // 2).transpose(0, 1, 3, 2, 4)
-    inputs1 = inputs1.reshape(rows, width // (2 * block), 2, block)
-    inputs2 = cross_inputs(z2, p2, block, 0)
-    inputs3 = cross_inputs(z3, p3, block, top_bit)
-    grad_now, grad_three = cross_backward(back, inputs3, factors[3], block, top_bit)
-    grad_now, grad_two = cross_backward(grad_now, inputs2, factors[2], block, 0)
-    grad_now, grad_one = second_backward(grad_now, inputs1, factors[1], block)
-    grad_now, grad_zero = first_backward(grad_now, inputs0, factors[0], block)
-    stacked = jnp.stack([grad_zero, grad_one, grad_two, grad_three])
-    stacked = lax.psum(stacked, "dp")
-    return (projected, grad_now, stacked)
 
 
 def solution(mesh):

time: 433 us -> 157 us (0.36)
  waiting for transfers between devices: 272 us -> 0 us
  Pallas kernels: 114 us -> 153 us
  between operations: 14.3 us -> 0.66 us
  local copies, waits for them, and re-layouts: 16.6 us -> 3.9 us
  matrix products: 11.4 us -> 0 us
    psum x1 -> x0, waiting for transfers between devices: 268 us -> none  [per_device(): stacked = lax.psum(stacked, 'dp')]
    pallas_call x1, Pallas kernels: 114 us -> 153 us  [per_device(): pl.pallas_call(main_kernel, out_shape=(jax.ShapeDtypeStruct((512, 896), B...]
    dot_general x8 -> x0, matrix products: 11.4 us -> none  [the longest x2 5.93 us: cross_backward(): jnp.einsum('thk,thw->khw', inputs, viewed, precision=HIGH)]
    pallas_call x6 -> x0, local copies, waits for them, and re-layouts: 7.01 us -> none  [main_call(): pl.pallas_call(main_kernel, out_shape=(jax.ShapeDtypeStruct((512, 896), B...]
  transfers between devices with their start and end apart: 3 -> 0, of which waited for: 3 -> 0; matrix products, arithmetic and copies ran while one was open for 3% -> 0% of each run, Pallas kernels for 0% -> 0%
where the time goes in v2:
time: 157 us
  Pallas kernels  153 us (97%)
  local copies, waits for them, and re-layouts  3.9 us (2%)
    pallas_call x1, Pallas kernels, per_device(): pl.pallas_call(main_kernel, out_shape=(jax.ShapeDtypeStruct((512, 896), B...  153 us
    unnamed x7, local copies, waits for them, and re-layouts  3.9 us

profile of v2, /device:TPU:1, one launch (start us, length us, event | category | flops | bytes accessed | tf_op | source)
XLA Modules:
  0.0 157.3 jit_solution(1369740231762424957)
XLA Ops:
  0.6 152.8 %rotate_project.1 = (bf16[512,896]{1,0:T(8,128)(2,1)}, f32[128,768]{1,0:T(8,128)}, f32[4,64,768]{2,1,0:T(8,128)}) custom-call(bf16[128,768]{1,0:T(8,128)(2,1)} %tokens.1, bf16[768,896]{1,0:T(8,128)(2,1)} %w_hbm.1, f32[4,64,768]{2,1,0:T(8,128)} %factors.1, bf16[768,896]{1,0:T(8,128)(2,1)} %w_hbm.1, bf16[512,896]{1,0:T(8,128)(2,1)} %cot_hbm.1), custom_call_target="tpu_custom_call" | custom-call | tf_op jit(solution)/shard_map/rotate_project/pallas_call | solution.py:465
  153.4 0.0 copy-start.1
  153.4 0.0 copy-start
  153.4 2.3 %copy.10 = bf16[512,896]{1,0:T(8,128)(2,1)} copy(bf16[512,896]{1,0:T(8,128)(2,1)} %get-tuple-element.6) | data formatting | bytes 1835008
  155.7 0.0 copy-done.1
  155.7 0.7 copy.11
  156.4 0.0 copy-done
  156.4 0.9 copy.12
Async XLA Ops:
  153.4 2.3 %copy-start.1 = (f32[128,768]{1,0:T(8,128)S(1)}, f32[128,768]{1,0:T(8,128)}, u32[]{:S(2)}) copy-start(f32[128,768]{1,0:T(8,128)} %get-tuple-element.7) | copy-start | bytes 1179652
  153.4 3.0 %copy-start = (f32[4,64,768]{2,1,0:T(8,128)S(1)}, f32[4,64,768]{2,1,0:T(8,128)}, u32[]{:S(2)}) copy-start(f32[4,64,768]{2,1,0:T(8,128)} %get-tuple-element.8) | copy-start | bytes 2359300

commit v3 on v0

v3 whole, which is shorter than its diff:
```python
import jax
import jax.numpy as jnp
from jax import lax
from jax.experimental import pallas as pl
from jax.experimental.pallas import tpu as pltpu
from jax.sharding import PartitionSpec as P

HIGH = lax.Precision.HIGHEST
F32 = jnp.float32
BF16 = jnp.bfloat16
MESH = pl.DeviceIdType.MESH
Q = [pl.ds(128 * q, 128) for q in range(6)]
H = [pl.ds(64 * h, 64) for h in range(2)]
M0, M1, OWN2, OTHER2, OWN3, OTHER3 = range(6)


def hdot(a, b, dims=((1,), (0,))):
    return lax.dot_general(a, b, (dims, ((), ())), precision=HIGH, preferred_element_type=F32)


def hdot_nt(a, b):
    return hdot(a, b, ((1,), (1,)))


def hdot_tn(a, b):
    return hdot(a, b, ((0,), (0,)))


def block_masks():
    r = lax.broadcasted_iota(jnp.int32, (128, 128), 0) // 32
    c = lax.broadcasted_iota(jnp.int32, (128, 128), 1) // 32
    return (r // 2 == c // 2, r % 2 == c % 2, r == c)


def fold_cross(full, masks):
    full = jnp.where(masks[2], full, 0.0)
    return full[:32] + full[32:64] + full[64:96] + full[96:]


def main_kernel(
    tokens_hbm, factors_hbm, w_hbm, cot_hbm,
    proj_hbm, grad_tokens_hbm, grad_factors_hbm,
    tokens, factors, proj, grad_factors, w_own, mats, z1, z2, p2, z3, p3, ga, gb, gc, gf, cin, gh, ghb, ain, res, fout,
    zsend, rot, R, cotG, w_oth, bsib, bsib_in, bown, up_out, up_in, dn_out, dn_in,
    pbuf, px_out, px_in, gsend, gin,
    loc_sem, sx, rx, sy, ry, sc, rc, sw, rw, sys, yr, sR, rR, sS, rS, sB, rB, sZ, rZ, sP, rP,
    sG, rG, sC, rC, sA, rA, sF, rF, sH, rH,
):
    dp, tn = lax.axis_index("dp"), lax.axis_index("tensor")
    core, z, yh = dp % 2, dp // 2 % 8, dp // 16
    x, yl = tn % 4, tn // 4
    chip = yh * 8 + z

    def dev(yh=yh, z=z, core=core, yl=yl, x=x):
        return (yh * 16 + z * 2 + core, yl * 4 + x)

    def chip_dev(index):
        return dev(yh=index // 8, z=index % 8)

    xl, xr, xo = (x + 3) % 4, (x + 1) % 4, (x + 2) % 4
    right, left = dev(x=xr), dev(x=xl)
    xpair = dev(x=x + 1 - 2 * (x % 2))
    ypair = dev(yl=1 - yl)
    sibling = dev(core=1 - core)
    above, below = dev(z=(z + 1) % 8), dev(z=(z + 7) % 8)
    diagonal = yh == yl
    off_diagonal = jnp.logical_not(diagonal)

    def rcopy(src, dst, ssem, rsem, to):
        return pltpu.make_async_remote_copy(
            src_ref=src, dst_ref=dst, send_sem=ssem, recv_sem=rsem,
            device_id=to, device_id_type=MESH,
        )

    def send(src, dst, ssem, rsem, to):
        rcopy(src, dst, ssem, rsem, to).start()

    def arrived(dst, rsem):
        rcopy(dst, dst, rsem, rsem, sibling).wait_recv()

    def all_sent(same_bytes, ssem):
        rcopy(same_bytes, same_bytes, ssem, ssem, sibling).wait_send()

    def local(src, dst, n):
        return pltpu.make_async_copy(src, dst, loc_sem.at[n])

    first = [local(tokens_hbm, tokens, 0), local(factors_hbm, factors, 1)]
    for copy in first:
        copy.start()

    barrier = pltpu.get_barrier_semaphore()

    def greet(r, carry):
        pl.semaphore_signal(barrier, inc=1, device_id=chip_dev((chip + r) % 16), device_id_type=MESH)
        return carry

    lax.fori_loop(1, 16, greet, 0)
    for peer in (right, left, ypair, sibling):
        pl.semaphore_signal(barrier, inc=1, device_id=peer, device_id_type=MESH)
    for peer, here in (
        (dev(yh=0, yl=yh), (yh == 0) & diagonal),
        (dev(yh=1, yl=yh), (yh == 1) & diagonal),
        (dev(yh=yl, yl=0), (yl == 0) & diagonal),
        (dev(yh=yl, yl=1), (yl == 1) & diagonal),
    ):
        @pl.when(jnp.logical_not(here))
        def _():
            pl.semaphore_signal(barrier, inc=1, device_id=peer, device_id_type=MESH)

    own_cot = [local(cot_hbm.at[pl.ds(256 * i, 256)], cotG.at[2 * x + i], 2 + i) for i in range(2)]
    own_w = local(w_hbm, w_own, 4)
    own_w.start()
    for copy in own_cot:
        copy.start()
    for copy in first:
        copy.wait()

    masks = block_masks()
    for q, cols in enumerate(Q):
        c0, c1 = factors[0, :, cols], factors[1, :, cols]
        mats[M0, q] = jnp.where(masks[0], jnp.concatenate([c0, c0], 0), 0.0)
        mats[M1, q] = jnp.where(
            masks[1], jnp.concatenate([c1[:32], c1[:32], c1[32:], c1[32:]], 0), 0.0
        )
        for section, bit, own in ((2, x % 2, OWN2), (3, yl, OWN3)):
            for part, place in ((bit, own), (1 - bit, own + 1)):
                coeffs = factors[section, pl.ds(32 * part, 32), cols]
                mats[place, q] = jnp.where(masks[2], jnp.concatenate([coeffs] * 4, 0), 0.0)
    for q, cols in enumerate(Q):
        field = tokens[:, cols].astype(F32)
        field = field + hdot(field, mats[M0, q])
        z1[:, cols] = field
        field = field + hdot(field, mats[M1, q])
        z2[:, cols] = field
        zsend[0, :, cols] = field.astype(BF16)

    pl.semaphore_wait(barrier, 23 - 2 * diagonal.astype(jnp.int32))

    def send_w(i):
        rows = pl.ds(128 * i, 128)
        send(w_hbm.at[rows], w_oth.at[rows], sw, rw, ypair)

    for h in range(2):
        send(zsend.at[0, H[h]], zsend.at[2, H[h]], sx, rx.at[h], xpair)
    send_w(0)
    for h in range(2):
        arrived(zsend.at[2, H[h]], rx.at[h])
        for q, cols in enumerate(Q):
            theirs = zsend[2, H[h], cols].astype(F32)
            p2[H[h], cols] = theirs
            field = z2[H[h], cols]
            field = field + hdot(field, mats[OWN2, q]) + hdot(theirs, mats[OTHER2, q])
            z3[H[h], cols] = field
            zsend[1, H[h], cols] = field.astype(BF16)
        send(zsend.at[1, H[h]], zsend.at[3, H[h]], sy, ry.at[h], ypair)

    for i, to in ((0, right), (1, left), (1, right), (0, left)):
        n = i + (0 if to is right else 2)
        send(cot_hbm.at[pl.ds(256 * i, 256)], cotG.at[2 * x + i], sc, rc.at[n], to)

    slot = (yl + yh) % 2

    def to_holder(b, h):
        src = rot.at[H[h]]
        dst = R.at[z, slot, core, H[h]]
        return rcopy(src, dst, sys.at[b], yr.at[slot, h], dev(yh=b, yl=yh))

    for h in range(2):
        arrived(zsend.at[3, H[h]], ry.at[h])
        for q, cols in enumerate(Q):
            theirs = zsend[3, H[h], cols].astype(F32)
            p3[H[h], cols] = theirs
            field = z3[H[h], cols]
            field = field + hdot(field, mats[OWN3, q]) + hdot(theirs, mats[OTHER3, q])
            rot[H[h], cols] = field.astype(BF16)
        for b in range(2):
            pl.when(jnp.logical_not((yh == b) & diagonal))(to_holder(b, h).start)

    @pl.when(diagonal)
    def _():
        R[z, 0, core] = rot[...]

    def spread(zz, s, up, down, k):
        block = R.at[zz, s, core]
        if up:
            send(block, block, sR.at[0], rR.at[0, k, s], above)
        if down:
            send(block, block, sR.at[1], rR.at[1, k, s], below)
        send(block, block, sS, rS, sibling)

    @pl.when(off_diagonal)
    def _():
        for h in range(2):
            arrived(R.at[z, 0, core, H[h]], yr.at[0, h])
    spread(z, 0, True, True, 0)
    for h in range(2):
        arrived(R.at[z, 1, core, H[h]], yr.at[1, h])
    spread(z, 1, True, True, 0)
    for i in range(1, 6):
        send_w(i)

    arrived(cotG.at[2 * xl], rc.at[0])
    send(cotG.at[2 * xl], cotG.at[2 * xl], sc, rc.at[4], right)
    arrived(cotG.at[2 * xr + 1], rc.at[3])
    send(cotG.at[2 * xr + 1], cotG.at[2 * xr + 1], sc, rc.at[5], left)

    def step(k):
        lo, hi = (z + 8 - k) % 8, (z + k) % 8
        for s in range(2):
            arrived(R.at[lo, s, core], rR.at[0, k - 1, s])
            spread(lo, s, k < 3 or s == 0, False, k)
            arrived(R.at[hi, s, core], rR.at[1, k - 1, s])
            spread(hi, s, False, k < 3 or s == 1, k)

    def sib_copy(zz, s):
        return rcopy(bsib.at[zz, s], bsib_in.at[zz, s], sB, rB.at[zz, s], sibling)

    def back_unit(xb, s):
        rows = cotG[pl.ds(2 * xb, 2)].reshape(512, 896)
        w = w_oth if s else w_own
        part = lax.dot_general(rows, w[...], (((1,), (1,)), ((), ())), preferred_element_type=F32)
        for c in range(2):
            @pl.when(core == c)
            def _():
                for i in range(2):
                    first, second = 256 * i + 128 * c, 256 * i + 128 * (1 - c)
                    bown[2 * xb + i, s] = part[first:first + 128]
                    bsib[2 * xb + i, s] = part[second:second + 128].astype(BF16)
        for i in range(2):
            sib_copy(2 * xb + i, s).start()

    for copy in own_cot:
        copy.wait()
    own_w.wait()
    back_unit(x, 0)
    step(1)
    arrived(cotG.at[2 * xl + 1], rc.at[1])
    back_unit(xl, 0)
    arrived(cotG.at[2 * xr], rc.at[2])
    back_unit(xr, 0)
    step(2)
    arrived(cotG.at[2 * xo], rc.at[4])
    arrived(cotG.at[2 * xo + 1], rc.at[5])
    back_unit(xo, 0)
    step(3)

    def back_ready(zz, s):
        arrived(bsib_in.at[zz, s], rB.at[zz, s])

    def own_back(zz, s, rows=slice(None)):
        return bown[zz, s, rows] + bsib_in[zz, s, rows].astype(F32)

    def ring_send(direction, n, zz, s, incoming, h=None):
        out, into = (up_out, up_in) if direction == 0 else (dn_out, dn_in)
        rows = slice(None) if h is None else H[h]
        value = own_back(zz, s, rows)
        if incoming is not None:
            if not h:
                arrived(into.at[incoming], rZ.at[direction, incoming, 0])
            value = value + into[incoming, rows].astype(F32)
        out[n, rows] = value.astype(BF16)
        src, dst = (out.at[n], into.at[n]) if h is None else (out.at[n, rows], into.at[n, rows])
        send(src, dst, sZ.at[direction], rZ.at[direction, n, h or 0], below if direction else above)

    def z_at(k):
        return (z + 8 + k) % 8

    back_ready(z_at(4), 0)
    ring_send(0, 0, z_at(4), 0, None)
    back_ready(z_at(-3), 0)
    ring_send(1, 1, z_at(-3), 0, None)

    arrived(w_oth, rw)
    far = z_at(4) // 2
    turn = 2 * (z % 2) - 1
    back_unit(far, 1)
    back_ready(z_at(4), 1)
    ring_send(1, 0, z_at(4), 1, None)
    back_unit((far + 4 + turn) % 4, 1)
    back_ready(z_at(3), 1)
    ring_send(0, 1, z_at(3), 1, None)

    zf = z_at(4)
    arrived(R.at[zf, 0, core], rR.at[0, 3, 0])
    spread(zf, 0, False, False, 4)
    arrived(R.at[zf, 1, core], rR.at[1, 3, 1])
    spread(zf, 1, False, False, 4)

    arrived(bsib, rS)

    def product(zz):
        return jnp.dot(R[zz, 0].reshape(256, 768), w_own[...], preferred_element_type=F32) + jnp.dot(
            R[zz, 1].reshape(256, 768), w_oth[...], preferred_element_type=F32
        )

    def px_send(direction, n, zz, incoming):
        value = product(zz)
        if incoming is not None:
            arrived(px_in.at[direction, incoming], rP.at[direction, incoming])
            value = value + px_in[direction, incoming].astype(F32)
        px_out[direction, n] = value.astype(BF16)
        send(px_out.at[direction, n], px_in.at[direction, n], sP, rP.at[direction, n], left if direction else right)

    px_send(0, 0, 2 * xo, None)
    px_send(1, 0, 2 * xo + 1, None)
    back_ready(z_at(3), 0)
    back_ready(z_at(-3), 1)
    ring_send(0, 2, z_at(3), 0, 0)
    ring_send(1, 2, z_at(-3), 1, 0)
    back_unit((far + 4 - turn) % 4, 1)
    back_unit((far + 2) % 4, 1)
    back_ready(z_at(2), 1)
    ring_send(0, 3, z_at(2), 1, 1)
    back_ready(z_at(-2), 0)
    ring_send(1, 3, z_at(-2), 0, 1)
    px_send(0, 1, 2 * xr + 1, None)
    px_send(1, 1, 2 * xl, None)
    back_ready(z_at(2), 0)
    ring_send(0, 4, z_at(2), 0, 2)
    back_ready(z_at(-2), 1)
    ring_send(1, 4, z_at(-2), 1, 2)
    back_ready(z_at(1), 1)
    back_ready(z_at(-1), 0)
    back_ready(z_at(1), 0)
    back_ready(z_at(-1), 1)
    for h in range(2):
        ring_send(0, 5, z_at(1), 1, 3, h)
        ring_send(1, 5, z_at(-1), 0, 3, h)
        ring_send(0, 6, z_at(1), 0, 4, h)
        ring_send(1, 6, z_at(-1), 1, 4, h)
    px_send(0, 2, 2 * xr, 0)
    px_send(1, 2, 2 * xl + 1, 0)
    back_ready(z, 0)
    back_ready(z, 1)
    pbuf[0] = product(2 * x)
    pbuf[1] = product(2 * x + 1)

    def to_owner(s, h):
        return rcopy(gsend.at[s, H[h]], gin.at[yh, H[h]], sG.at[s], rG.at[yh, h], dev(yh=yl, yl=(yl + s) % 2))

    for h in range(2):
        rows = H[h]
        for s, nu, nd in ((1, 5, 6), (0, 6, 5)):
            arrived(up_in.at[nu, rows], rZ.at[0, nu, h])
            arrived(dn_in.at[nd, rows], rZ.at[1, nd, h])
            total = own_back(z, s, rows) + up_in[nu, rows].astype(F32) + dn_in[nd, rows].astype(F32)
            gsend[s, rows] = total.astype(BF16)
            if s == 1:
                to_owner(s, h).start()
            else:
                pl.when(off_diagonal)(to_owner(s, h).start)

                @pl.when(diagonal)
                def _():
                    gin[yh, rows] = gsend[0, rows]

    def reduce_start(s):
        send(gf.at[s, pl.ds(32 * (1 - core), 32)], cin.at[s], sC, rC.at[s], sibling)

    def piece(j):
        return (pl.ds(16 * (j // 2), 16), pl.ds(384 * (j % 2), 384))

    def owner_of(s, j):
        return 8 * (j % 2) + 4 * (j // 2) + s

    def owner_copy(s, j):
        owner = owner_of(s, j)
        r = (chip + 16 - owner) % 16
        src = ghb.at[s, piece(j)[0], piece(j)[1]]
        return r, rcopy(src, ain.at[(r + 15) % 16], sA, rA, chip_dev(owner))

    def reduce_middle(s):
        arrived(cin.at[s], rC.at[s])
        gh[s] = gf[s, pl.ds(32 * core, 32), :] + cin[s]
        ghb[s] = gh[s].astype(BF16)
        for j in range(4):
            r, copy = owner_copy(s, j)
            pl.when(r != 0)(copy.start)

    own_s = z % 4
    own_rows, own_cols = pl.ds(16 * (z // 4), 16), pl.ds(384 * yh, 384)

    def peer_copy(r):
        place = fout.at[core, own_s, own_rows, own_cols]
        return rcopy(res, place, sF, rF.at[own_s], chip_dev((chip + r) % 16))

    def own_work():
        arrived(ain.at[pl.ds(0, 15)], rA)

        def add(r, total):
            return total + ain[r - 1].astype(F32)

        total = lax.fori_loop(1, 16, add, gh[own_s, own_rows, own_cols])
        res[...] = total.astype(BF16)
        fout[core, own_s, own_rows, own_cols] = res[...]

        def push(r, carry):
            peer_copy(r).start()
            return carry

        lax.fori_loop(1, 16, push, 0)

    def cross_out(g, h, other, a, ssem, rsem, peer):
        for q, cols in enumerate(Q):
            zsend[a, H[h], cols] = hdot_nt(g[H[h], cols], mats[other, q]).astype(BF16)
        send(zsend.at[a, H[h]], zsend.at[a + 1, H[h]], ssem, rsem, peer)

    def cross_kept(g, out, section, own, saved, partner, bit):
        for q, cols in enumerate(Q):
            field = g[:, cols]
            out[:, cols] = field + hdot_nt(field, mats[own, q])
            gf[section, pl.ds(32 * bit, 32), cols] = fold_cross(hdot_tn(saved[:, cols], field), masks)
            gf[section, pl.ds(32 * (1 - bit), 32), cols] = fold_cross(hdot_tn(partner[:, cols], field), masks)
        reduce_start(section)

    def cross_in(out, h, a, rsem):
        arrived(zsend.at[a + 1, H[h]], rsem)
        out[H[h]] += zsend[a + 1, H[h]].astype(F32)

    def local_back(g, out, section, saved):
        for q, cols in enumerate(Q):
            field = g[:, cols]
            out[:, cols] = field + hdot_nt(field, mats[section, q])
            full = jnp.where(masks[section], hdot_tn(saved[:, cols].astype(F32), field), 0.0)
            if section == 0:
                gf[0, :, cols] = full[:64] + full[64:]
            else:
                gf[1, pl.ds(0, 32), cols] = full[:32] + full[32:64]
                gf[1, pl.ds(32, 32), cols] = full[64:96] + full[96:]
        reduce_start(section)

    for h in range(2):
        for a in range(2):
            @pl.when(jnp.logical_not((yh == a) & diagonal))
            def _():
                arrived(gin.at[a, H[h]], rG.at[a, h])
        ga[H[h]] = gin[0, H[h]].astype(F32) + gin[1, H[h]].astype(F32)
        cross_out(ga, h, OTHER3, 4, sy, ry.at[2 + h], ypair)
    cross_kept(ga, gb, 3, OWN3, z3, p3, yl)
    for h in range(2):
        cross_in(gb, h, 4, ry.at[2 + h])
        cross_out(gb, h, OTHER2, 6, sx, rx.at[2 + h], xpair)
    cross_kept(gb, gc, 2, OWN2, z2, p2, x % 2)
    for h in range(2):
        cross_in(gc, h, 6, rx.at[2 + h])
    reduce_middle(3)
    local_back(gc, gb, 1, z1)
    local_back(gb, ga, 0, tokens)
    grad_tokens_out = local(ga, grad_tokens_hbm, 5)
    grad_tokens_out.start()
    reduce_middle(2)
    reduce_middle(1)
    reduce_middle(0)
    pl.when(own_s >= 2)(own_work)
    for i, nu, nd in ((0, 2, 1), (1, 1, 2)):
        arrived(px_in.at[0, nu], rP.at[0, nu])
        arrived(px_in.at[1, nd], rP.at[1, nd])
        total = pbuf[i] + px_in[0, nu].astype(F32) + px_in[1, nd].astype(F32)
        proj[pl.ds(256 * i, 256), :] = total.astype(BF16)

    proj_out = local(proj, proj_hbm, 6)
    proj_out.start()
    pl.when(own_s < 2)(own_work)
    for s in (3, 2, 1, 0):
        @pl.when(own_s != s)
        def _():
            arrived(ain.at[pl.ds(0, 4)], rF.at[s])

        @pl.when(own_s == s)
        def _():
            arrived(ain.at[pl.ds(0, 3)], rF.at[s])

        send(fout.at[core, s], fout.at[core, s], sH, rH.at[s], sibling)
        grad_factors[s, pl.ds(32 * core, 32), :] = fout[core, s].astype(F32)
    factors_out = [local(grad_factors.at[s], grad_factors_hbm.at[s], 7 + s) for s in range(4)]
    for s in (3, 2, 1, 0):
        arrived(fout.at[1 - core, s], rH.at[s])
        grad_factors[s, pl.ds(32 - 32 * core, 32), :] = fout[1 - core, s].astype(F32)
        factors_out[s].start()

    for copy in (grad_tokens_out, proj_out, *factors_out):
        copy.wait()
    all_sent(zsend.at[pl.ds(0, 2)], sx)
    all_sent(zsend.at[pl.ds(0, 2)], sy)
    all_sent(px_out, sc)
    all_sent(w_oth, sw)
    for b in range(2):
        pl.when(jnp.logical_not((yh == b) & diagonal))(lambda: all_sent(rot, sys.at[b]))
        all_sent(up_out, sR.at[b])
        all_sent(up_out, sZ.at[b])
    all_sent(bsib, sS)
    all_sent(bsib, sB)
    all_sent(px_out, sP)
    pl.when(off_diagonal)(lambda: all_sent(rot, sG.at[0]))
    all_sent(rot, sG.at[1])
    all_sent(cin, sC)
    all_sent(ain.at[pl.ds(0, 15)], sA)
    all_sent(ain.at[pl.ds(0, 15)], sF)
    all_sent(fout.at[0], sH)


def per_device(tokens, weight, factors, cotangent):
    V = pltpu.VMEM
    D = pltpu.SemaphoreType.DMA
    shapes = (
        jax.ShapeDtypeStruct((512, 896), BF16),
        jax.ShapeDtypeStruct((128, 768), F32),
        jax.ShapeDtypeStruct((4, 64, 768), F32),
    )
    hbm = pl.BlockSpec(memory_space=pl.ANY)
    return pl.pallas_call(
        main_kernel,
        out_shape=shapes,
        in_specs=[hbm] * 4,
        out_specs=(hbm,) * 3,
        scratch_shapes=[
            V((128, 768), BF16),
            V((4, 64, 768), F32),
            V((512, 896), BF16),
            V((4, 64, 768), F32),
            V((768, 896), BF16),
            V((6, 6, 128, 128), F32),
            *[V((128, 768), F32)] * 8,
            V((4, 64, 768), F32),
            V((4, 32, 768), F32),
            V((4, 32, 768), F32),
            V((4, 32, 768), BF16),
            V((16, 16, 384), BF16),
            V((16, 384), BF16),
            V((2, 4, 32, 768), BF16),
            V((8, 128, 768), BF16),
            V((128, 768), BF16),
            V((8, 2, 2, 128, 768), BF16),
            V((8, 256, 896), BF16),
            V((768, 896), BF16),
            V((8, 2, 128, 768), BF16),
            V((8, 2, 128, 768), BF16),
            V((8, 2, 128, 768), F32),
            *[V((7, 128, 768), BF16)] * 4,
            V((2, 256, 896), F32),
            V((2, 3, 256, 896), BF16),
            V((2, 3, 256, 896), BF16),
            V((2, 128, 768), BF16),
            V((2, 128, 768), BF16),
            D((11,)),
            D, D((4,)), D, D((4,)),
            D, D((6,)), D, D,
            D((2,)), D((2, 2)),
            D((2,)), D((2, 4, 2)),
            D, D,
            D, D((8, 2)),
            D((2,)), D((2, 7, 2)),
            D, D((2, 3)),
            D((2,)), D((2, 2)),
            D, D((4,)),
            D, D,
            D, D((4,)),
            D, D((4,)),
        ],
        compiler_params=pltpu.CompilerParams(
            collective_id=0, has_side_effects=True, vmem_limit_bytes=56 * 1024 * 1024
        ),
        name="rotate_project",
    )(tokens, factors, weight, cotangent)


def solution(mesh):
    placed = (P("dp", "tensor"), P("tensor", "dp"), P(None, None, "tensor"), P("tensor", "dp"))
    return jax.shard_map(
        per_device,
        mesh=mesh,
        in_specs=placed,
        out_specs=(P("tensor", "dp"), P("dp", "tensor"), P(None, None, "tensor")),
        check_vma=False,
    )
```

time: 816 us -> 131 us (0.16)
  waiting for transfers between devices: 725 us -> 0 us
  Pallas kernels: 0 us -> 127 us
  matrix products: 43.5 us -> 0 us
  local copies, waits for them, and re-layouts: 18.2 us -> 3.9 us
  between operations: 14.1 us -> 0.66 us
  other arithmetic: 12.3 us -> 0 us
    reduce_scatter x2 -> x0, waiting for transfers between devices: 292 us -> none  [the longest x1 153 us: per_device(): lax.psum_scatter(partial_out, 'tensor', scatter_dimension=0, tiled=True)]
    psum x1 -> x0, waiting for transfers between devices: 254 us -> none  [per_device(): stacked = lax.psum(stacked, 'dp')]
    all_gather x2 -> x0, waiting for transfers between devices: 157 us -> none  [the longest x1 90.3 us: per_device(): all_cotangent = lax.all_gather(cotangent, 'tensor', axis=0, tiled=True)]
    pallas_call x0 -> x1, Pallas kernels: none -> 127 us  [per_device(): pl.pallas_call(main_kernel, out_shape=shapes, in_specs=[hbm] * 4, out_spe...]
    dot_general x14 -> x0, matrix products: 43.5 us -> none  [the longest x1 12.4 us: per_device(): jnp.dot(lax.all_gather(rotated, 'dp', axis=0, tiled=True), weight, prefer...]
    ppermute x4 -> x0, waiting for transfers between devices: 21.6 us -> none  [swapped(): lax.ppermute(shard, axis, [(i, i ^ 1 << bit) for i in range(lax.axis_size...]
  transfers between devices with their start and end apart: 9 -> 0, of which waited for: 8 -> 0; matrix products, arithmetic and copies ran while one was open for 7% -> 0% of each run, Pallas kernels for 0% -> 0%
where the time goes in v3:
time: 131 us
  Pallas kernels  127 us (97%)
  local copies, waits for them, and re-layouts  3.9 us (3%)
    pallas_call x1, Pallas kernels, per_device(): pl.pallas_call(main_kernel, out_shape=shapes, in_specs=[hbm] * 4, out_spe...  127 us
    unnamed x7, local copies, waits for them, and re-layouts  3.9 us

profile of v3, /device:TPU:1, one launch (start us, length us, event | category | flops | bytes accessed | tf_op | source)
XLA Modules:
  0.0 131.1 jit_solution(14025974816988215847)
XLA Ops:
  0.6 126.5 %rotate_project.1 = (bf16[512,896]{1,0:T(8,128)(2,1)}, f32[128,768]{1,0:T(8,128)}, f32[4,64,768]{2,1,0:T(8,128)}) custom-call(bf16[128,768]{1,0:T(8,128)(2,1)} %tokens_hbm.1, f32[4,64,768]{2,1,0:T(8,128)} %factors_hbm.1, bf16[768,896]{1,0:T(8,128)(2,1)} %w_hbm.1, bf16[512,896]{1,0:T(8,128)(2,1)} %cot_hbm.1), custom_call_target="tpu_custom_call" | custom-call | tf_op jit(solution)/shard_map/rotate_project/pallas_call | solution.py:511
  127.2 0.0 copy-start.1
  127.2 0.0 copy-start
  127.2 2.3 %copy.10 = bf16[512,896]{1,0:T(8,128)(2,1)} copy(bf16[512,896]{1,0:T(8,128)(2,1)} %get-tuple-element.6) | data formatting | bytes 1835008
  129.5 0.0 copy-done.1
  129.5 0.7 copy.11
  130.2 0.0 copy-done
  130.2 0.9 copy.12
Async XLA Ops:
  127.2 2.3 %copy-start.1 = (f32[128,768]{1,0:T(8,128)S(1)}, f32[128,768]{1,0:T(8,128)}, u32[]{:S(2)}) copy-start(f32[128,768]{1,0:T(8,128)} %get-tuple-element.7) | copy-start | bytes 1179652
  127.2 3.0 %copy-start = (f32[4,64,768]{2,1,0:T(8,128)S(1)}, f32[4,64,768]{2,1,0:T(8,128)}, u32[]{:S(2)}) copy-start(f32[4,64,768]{2,1,0:T(8,128)} %get-tuple-element.8) | copy-start | bytes 2359300

commit v4 on v3

--- a/solution.py
+++ b/solution.py
@@ -142,6 +142,9 @@
 
     for h in range(2):
         send(zsend.at[0, H[h]], zsend.at[2, H[h]], sx, rx.at[h], xpair)
+    for i, to in ((0, right), (1, left), (1, right), (0, left)):
+        n = i + (0 if to is right else 2)
+        send(cot_hbm.at[pl.ds(256 * i, 256)], cotG.at[2 * x + i], sc, rc.at[n], to)
     send_w(0)
     for h in range(2):
         arrived(zsend.at[2, H[h]], rx.at[h])
@@ -154,10 +157,6 @@
             zsend[1, H[h], cols] = field.astype(BF16)
         send(zsend.at[1, H[h]], zsend.at[3, H[h]], sy, ry.at[h], ypair)
 
-    for i, to in ((0, right), (1, left), (1, right), (0, left)):
-        n = i + (0 if to is right else 2)
-        send(cot_hbm.at[pl.ds(256 * i, 256)], cotG.at[2 * x + i], sc, rc.at[n], to)
-
     slot = (yl + yh) % 2
 
     def to_holder(b, h):
@@ -186,7 +185,7 @@
             send(block, block, sR.at[0], rR.at[0, k, s], above)
         if down:
             send(block, block, sR.at[1], rR.at[1, k, s], below)
-        send(block, block, sS, rS, sibling)
+        send(block, block, sS, rS.at[int(k > 2)], sibling)
 
     @pl.when(off_diagonal)
     def _():
@@ -204,13 +203,13 @@
     arrived(cotG.at[2 * xr + 1], rc.at[3])
     send(cotG.at[2 * xr + 1], cotG.at[2 * xr + 1], sc, rc.at[5], left)
 
-    def step(k):
+    def step(k, onward):
         lo, hi = (z + 8 - k) % 8, (z + k) % 8
         for s in range(2):
             arrived(R.at[lo, s, core], rR.at[0, k - 1, s])
-            spread(lo, s, k < 3 or s == 0, False, k)
+            spread(lo, s, onward or s == 0, False, k)
             arrived(R.at[hi, s, core], rR.at[1, k - 1, s])
-            spread(hi, s, False, k < 3 or s == 1, k)
+            spread(hi, s, False, onward or s == 0, k)
 
     def sib_copy(zz, s):
         return rcopy(bsib.at[zz, s], bsib_in.at[zz, s], sB, rB.at[zz, s], sibling)
@@ -233,126 +232,144 @@
         copy.wait()
     own_w.wait()
     back_unit(x, 0)
-    step(1)
+    step(1, True)
     arrived(cotG.at[2 * xl + 1], rc.at[1])
     back_unit(xl, 0)
     arrived(cotG.at[2 * xr], rc.at[2])
     back_unit(xr, 0)
-    step(2)
+    step(2, False)
     arrived(cotG.at[2 * xo], rc.at[4])
     arrived(cotG.at[2 * xo + 1], rc.at[5])
     back_unit(xo, 0)
-    step(3)
-
-    def back_ready(zz, s):
-        arrived(bsib_in.at[zz, s], rB.at[zz, s])
-
-    def own_back(zz, s, rows=slice(None)):
-        return bown[zz, s, rows] + bsib_in[zz, s, rows].astype(F32)
-
-    def ring_send(direction, n, zz, s, incoming, h=None):
-        out, into = (up_out, up_in) if direction == 0 else (dn_out, dn_in)
-        rows = slice(None) if h is None else H[h]
-        value = own_back(zz, s, rows)
-        if incoming is not None:
-            if not h:
-                arrived(into.at[incoming], rZ.at[direction, incoming, 0])
-            value = value + into[incoming, rows].astype(F32)
-        out[n, rows] = value.astype(BF16)
-        src, dst = (out.at[n], into.at[n]) if h is None else (out.at[n, rows], into.at[n, rows])
-        send(src, dst, sZ.at[direction], rZ.at[direction, n, h or 0], below if direction else above)
 
     def z_at(k):
         return (z + 8 + k) % 8
 
-    back_ready(z_at(4), 0)
-    ring_send(0, 0, z_at(4), 0, None)
-    back_ready(z_at(-3), 0)
-    ring_send(1, 1, z_at(-3), 0, None)
-
+    def back_ready(s, *places):
+        for k in places:
+            arrived(bsib_in.at[z_at(k), s], rB.at[z_at(k), s])
+
+    def own_back(zz, s, rows):
+        return bown[zz, s, rows] + bsib_in[zz, s, rows].astype(F32)
+
+    def ring_send(s, n):
+        for direction in range(2):
+            out, into = (dn_out, dn_in) if direction else (up_out, up_in)
+            distance = 4 - (n + 1) // 2
+            h = direction if n % 2 == 0 else 1 - direction
+            value = own_back(z_at(-distance if direction else distance), s, H[h])
+            if n >= 2:
+                arrived(into.at[7 * s + n - 2], rZ.at[direction, 7 * s + n - 2])
+                value = value + into[7 * s + n - 2].astype(F32)
+            m = 7 * s + n
+            out[m] = value.astype(BF16)
+            send(out.at[m], into.at[m], sZ.at[direction], rZ.at[direction, m], below if direction else above)
+
+    def to_owner(s, h):
+        return rcopy(gsend.at[s, H[h]], gin.at[yh, H[h]], sG.at[s], rG.at[yh, h], dev(yh=yl, yl=(yl + s) % 2))
+
+    def ring_end(s):
+        for h in (1, 0):
+            nu, nd = 7 * s + 6 - h, 7 * s + 5 + h
+            arrived(up_in.at[nu], rZ.at[0, nu])
+            arrived(dn_in.at[nd], rZ.at[1, nd])
+            total = own_back(z, s, H[h]) + up_in[nu].astype(F32) + dn_in[nd].astype(F32)
+            gsend[s, H[h]] = total.astype(BF16)
+            if s == 1:
+                to_owner(s, h).start()
+            else:
+                pl.when(off_diagonal)(to_owner(s, h).start)
+
+                @pl.when(diagonal)
+                def _():
+                    gin[yh, H[h]] = gsend[0, H[h]]
+
+    def product(zz):
+        return jnp.dot(R[zz, 0].reshape(256, 768), w_own[...], preferred_element_type=F32) + jnp.dot(
+            R[zz, 1].reshape(256, 768), w_oth[...], preferred_element_type=F32
+        )
+
+    def in_phase(zz, late):
+        away = (zz - z + 8) % 8
+        return ((away >= 3) & (away <= 5)) == late
+
+    def px_send(late, n, after_far=None):
+        for direction in range(2):
+            zz = ((2 * xo + 1, 2 * xr, 2 * xr + 1), (2 * xo, 2 * xl + 1, 2 * xl))[direction][n]
+            now = in_phase(zz, late)
+            if after_far is not None:
+                now = now & in_phase(2 * xo + 1 - direction, after_far)
+
+            @pl.when(now)
+            def _():
+                value = product(zz)
+                if n == 2:
+                    arrived(px_in.at[direction, 0], rP.at[direction, 0])
+                    value = value + px_in[direction, 0].astype(F32)
+                px_out[direction, n] = value.astype(BF16)
+                send(
+                    px_out.at[direction, n], px_in.at[direction, n], sP, rP.at[direction, n],
+                    left if direction else right,
+                )
+
+    def px_own(late):
+        for i in range(2):
+            @pl.when(in_phase(2 * x + i, late))
+            def _():
+                pbuf[i] = product(2 * x + i)
+
+    def third_step(s):
+        lo, hi = z_at(-3), z_at(3)
+        arrived(R.at[lo, s, core], rR.at[0, 2, s])
+        spread(lo, s, False, False, 3)
+        arrived(R.at[hi, s, core], rR.at[1, 2, s])
+        spread(hi, s, False, s == 1, 3)
+
+    def last_step():
+        zf = z_at(4)
+        for s in range(2):
+            arrived(R.at[zf, s, core], rR.at[s, 3, s])
+            spread(zf, s, False, False, 4)
+
+    back_ready(0, 4, 3, -3)
+    ring_send(0, 0)
+    ring_send(0, 1)
+    back_ready(0, 2, -2, 1, -1, 0)
+    ring_send(0, 2)
+    ring_send(0, 3)
     arrived(w_oth, rw)
     far = z_at(4) // 2
     turn = 2 * (z % 2) - 1
     back_unit(far, 1)
-    back_ready(z_at(4), 1)
-    ring_send(1, 0, z_at(4), 1, None)
+    ring_send(0, 4)
+    arrived(R.at[pl.ds(0, 5), :, 0], rS.at[0])
+    px_send(False, 0)
+    ring_send(0, 5)
     back_unit((far + 4 + turn) % 4, 1)
-    back_ready(z_at(3), 1)
-    ring_send(0, 1, z_at(3), 1, None)
-
-    zf = z_at(4)
-    arrived(R.at[zf, 0, core], rR.at[0, 3, 0])
-    spread(zf, 0, False, False, 4)
-    arrived(R.at[zf, 1, core], rR.at[1, 3, 1])
-    spread(zf, 1, False, False, 4)
-
-    arrived(bsib, rS)
-
-    def product(zz):
-        return jnp.dot(R[zz, 0].reshape(256, 768), w_own[...], preferred_element_type=F32) + jnp.dot(
-            R[zz, 1].reshape(256, 768), w_oth[...], preferred_element_type=F32
-        )
-
-    def px_send(direction, n, zz, incoming):
-        value = product(zz)
-        if incoming is not None:
-            arrived(px_in.at[direction, incoming], rP.at[direction, incoming])
-            value = value + px_in[direction, incoming].astype(F32)
-        px_out[direction, n] = value.astype(BF16)
-        send(px_out.at[direction, n], px_in.at[direction, n], sP, rP.at[direction, n], left if direction else right)
-
-    px_send(0, 0, 2 * xo, None)
-    px_send(1, 0, 2 * xo + 1, None)
-    back_ready(z_at(3), 0)
-    back_ready(z_at(-3), 1)
-    ring_send(0, 2, z_at(3), 0, 0)
-    ring_send(1, 2, z_at(-3), 1, 0)
+    ring_send(0, 6)
+    back_ready(1, 4, 3, -3)
+    ring_send(1, 0)
+    ring_send(1, 1)
     back_unit((far + 4 - turn) % 4, 1)
+    third_step(0)
     back_unit((far + 2) % 4, 1)
-    back_ready(z_at(2), 1)
-    ring_send(0, 3, z_at(2), 1, 1)
-    back_ready(z_at(-2), 0)
-    ring_send(1, 3, z_at(-2), 0, 1)
-    px_send(0, 1, 2 * xr + 1, None)
-    px_send(1, 1, 2 * xl, None)
-    back_ready(z_at(2), 0)
-    ring_send(0, 4, z_at(2), 0, 2)
-    back_ready(z_at(-2), 1)
-    ring_send(1, 4, z_at(-2), 1, 2)
-    back_ready(z_at(1), 1)
-    back_ready(z_at(-1), 0)
-    back_ready(z_at(1), 0)
-    back_ready(z_at(-1), 1)
-    for h in range(2):
-        ring_send(0, 5, z_at(1), 1, 3, h)
-        ring_send(1, 5, z_at(-1), 0, 3, h)
-        ring_send(0, 6, z_at(1), 0, 4, h)
-        ring_send(1, 6, z_at(-1), 1, 4, h)
-    px_send(0, 2, 2 * xr, 0)
-    px_send(1, 2, 2 * xl + 1, 0)
-    back_ready(z, 0)
-    back_ready(z, 1)
-    pbuf[0] = product(2 * x)
-    pbuf[1] = product(2 * x + 1)
-
-    def to_owner(s, h):
-        return rcopy(gsend.at[s, H[h]], gin.at[yh, H[h]], sG.at[s], rG.at[yh, h], dev(yh=yl, yl=(yl + s) % 2))
-
-    for h in range(2):
-        rows = H[h]
-        for s, nu, nd in ((1, 5, 6), (0, 6, 5)):
-            arrived(up_in.at[nu, rows], rZ.at[0, nu, h])
-            arrived(dn_in.at[nd, rows], rZ.at[1, nd, h])
-            total = own_back(z, s, rows) + up_in[nu, rows].astype(F32) + dn_in[nd, rows].astype(F32)
-            gsend[s, rows] = total.astype(BF16)
-            if s == 1:
-                to_owner(s, h).start()
-            else:
-                pl.when(off_diagonal)(to_owner(s, h).start)
-
-                @pl.when(diagonal)
-                def _():
-                    gin[yh, rows] = gsend[0, rows]
+    ring_send(1, 2)
+    ring_end(0)
+    back_ready(1, 2, -2)
+    ring_send(1, 3)
+    px_send(False, 1)
+    ring_send(1, 4)
+    back_ready(1, 1, -1, 0)
+    ring_send(1, 5)
+    px_own(False)
+    ring_send(1, 6)
+    held = ((z_at(-2), 1, 0, 2, above), (z_at(2), 1, 1, 2, below), (z_at(-3), 0, 0, 3, above))
+    for zz, s, direction, k, to in held:
+        block = R.at[zz, s, core]
+        send(block, block, sR.at[direction], rR.at[direction, k, s], to)
+    px_send(False, 2)
+    ring_end(1)
+    third_step(1)
 
     def reduce_start(s):
         send(gf.at[s, pl.ds(32 * (1 - core), 32)], cin.at[s], sC, rC.at[s], sibling)
@@ -437,10 +454,14 @@
         ga[H[h]] = gin[0, H[h]].astype(F32) + gin[1, H[h]].astype(F32)
         cross_out(ga, h, OTHER3, 4, sy, ry.at[2 + h], ypair)
     cross_kept(ga, gb, 3, OWN3, z3, p3, yl)
+    last_step()
     for h in range(2):
         cross_in(gb, h, 4, ry.at[2 + h])
         cross_out(gb, h, OTHER2, 6, sx, rx.at[2 + h], xpair)
     cross_kept(gb, gc, 2, OWN2, z2, p2, x % 2)
+    arrived(R.at[pl.ds(0, 3), :, 0], rS.at[1])
+    px_send(True, 0)
+    px_send(True, 1, False)
     for h in range(2):
         cross_in(gc, h, 6, rx.at[2 + h])
     reduce_middle(3)
@@ -451,16 +472,11 @@
     reduce_middle(2)
     reduce_middle(1)
     reduce_middle(0)
+    px_send(True, 1, True)
     pl.when(own_s >= 2)(own_work)
-    for i, nu, nd in ((0, 2, 1), (1, 1, 2)):
-        arrived(px_in.at[0, nu], rP.at[0, nu])
-        arrived(px_in.at[1, nd], rP.at[1, nd])
-        total = pbuf[i] + px_in[0, nu].astype(F32) + px_in[1, nd].astype(F32)
-        proj[pl.ds(256 * i, 256), :] = total.astype(BF16)
-
-    proj_out = local(proj, proj_hbm, 6)
-    proj_out.start()
+    px_send(True, 2)
     pl.when(own_s < 2)(own_work)
+    px_own(True)
     for s in (3, 2, 1, 0):
         @pl.when(own_s != s)
         def _():
@@ -478,6 +494,14 @@
         grad_factors[s, pl.ds(32 - 32 * core, 32), :] = fout[1 - core, s].astype(F32)
         factors_out[s].start()
 
+    for i, nu, nd in ((0, 1, 2), (1, 2, 1)):
+        arrived(px_in.at[0, nu], rP.at[0, nu])
+        arrived(px_in.at[1, nd], rP.at[1, nd])
+        total = pbuf[i] + px_in[0, nu].astype(F32) + px_in[1, nd].astype(F32)
+        proj[pl.ds(256 * i, 256), :] = total.astype(BF16)
+
+    proj_out = local(proj, proj_hbm, 6)
+    proj_out.start()
     for copy in (grad_tokens_out, proj_out, *factors_out):
         copy.wait()
     all_sent(zsend.at[pl.ds(0, 2)], sx)
@@ -536,7 +560,7 @@
             V((8, 2, 128, 768), BF16),
             V((8, 2, 128, 768), BF16),
             V((8, 2, 128, 768), F32),
-            *[V((7, 128, 768), BF16)] * 4,
+            *[V((14, 64, 768), BF16)] * 4,
             V((2, 256, 896), F32),
             V((2, 3, 256, 896), BF16),
             V((2, 3, 256, 896), BF16),
@@ -547,9 +571,9 @@
             D, D((6,)), D, D,
             D((2,)), D((2, 2)),
             D((2,)), D((2, 4, 2)),
-            D, D,
+            D, D((2,)),
             D, D((8, 2)),
-            D((2,)), D((2, 7, 2)),
+            D((2,)), D((2, 14)),
             D, D((2, 3)),
             D((2,)), D((2, 2)),
             D, D((4,)),

time: 131 us -> 126 us (0.962)
  Pallas kernels: 127 us -> 122 us
    pallas_call x1, Pallas kernels: 127 us -> 122 us  [per_device(): pl.pallas_call(main_kernel, out_shape=shapes, in_specs=[hbm] * 4, out_spe...]
where the time goes in v4:
time: 126 us
  Pallas kernels  122 us (97%)
  local copies, waits for them, and re-layouts  3.9 us (3%)
    pallas_call x1, Pallas kernels, per_device(): pl.pallas_call(main_kernel, out_shape=shapes, in_specs=[hbm] * 4, out_spe...  122 us
    unnamed x7, local copies, waits for them, and re-layouts  3.9 us

profile of v4, /device:TPU:1, one launch (start us, length us, event | category | flops | bytes accessed | tf_op | source)
XLA Modules:
  0.0 126.3 jit_solution(14146958488521271417)
XLA Ops:
  0.6 121.8 %rotate_project.1 = (bf16[512,896]{1,0:T(8,128)(2,1)}, f32[128,768]{1,0:T(8,128)}, f32[4,64,768]{2,1,0:T(8,128)}) custom-call(bf16[128,768]{1,0:T(8,128)(2,1)} %tokens_hbm.1, f32[4,64,768]{2,1,0:T(8,128)} %factors_hbm.1, bf16[768,896]{1,0:T(8,128)(2,1)} %w_hbm.1, bf16[512,896]{1,0:T(8,128)(2,1)} %cot_hbm.1), custom_call_target="tpu_custom_call" | custom-call | tf_op jit(solution)/shard_map/rotate_project/pallas_call | solution.py:535
  122.4 0.0 copy-start.1
  122.4 0.0 copy-start
  122.4 2.3 %copy.10 = bf16[512,896]{1,0:T(8,128)(2,1)} copy(bf16[512,896]{1,0:T(8,128)(2,1)} %get-tuple-element.6) | data formatting | bytes 1835008
  124.7 0.0 copy-done.1
  124.7 0.7 copy.11
  125.4 0.0 copy-done
  125.5 0.9 copy.12
Async XLA Ops:
  122.4 2.3 %copy-start.1 = (f32[128,768]{1,0:T(8,128)S(1)}, f32[128,768]{1,0:T(8,128)}, u32[]{:S(2)}) copy-start(f32[128,768]{1,0:T(8,128)} %get-tuple-element.7) | copy-start | bytes 1179652
  122.4 3.0 %copy-start = (f32[4,64,768]{2,1,0:T(8,128)S(1)}, f32[4,64,768]{2,1,0:T(8,128)}, u32[]{:S(2)}) copy-start(f32[4,64,768]{2,1,0:T(8,128)} %get-tuple-element.8) | copy-start | bytes 2359300

commit v5 on v4

--- a/solution.py
+++ b/solution.py
@@ -5,25 +5,24 @@
 from jax.experimental.pallas import tpu as pltpu
 from jax.sharding import PartitionSpec as P
 
-HIGH = lax.Precision.HIGHEST
 F32 = jnp.float32
 BF16 = jnp.bfloat16
 MESH = pl.DeviceIdType.MESH
 Q = [pl.ds(128 * q, 128) for q in range(6)]
+U = [pl.ds(256 * u, 256) for u in range(3)]
 H = [pl.ds(64 * h, 64) for h in range(2)]
+PX = [pl.ds(128 * h, 128) for h in range(2)]
 M0, M1, OWN2, OTHER2, OWN3, OTHER3 = range(6)
-
-
-def hdot(a, b, dims=((1,), (0,))):
-    return lax.dot_general(a, b, (dims, ((), ())), precision=HIGH, preferred_element_type=F32)
-
-
-def hdot_nt(a, b):
-    return hdot(a, b, ((1,), (1,)))
-
-
-def hdot_tn(a, b):
-    return hdot(a, b, ((0,), (0,)))
+T0, T1, T2, T3, P2, P3 = 0, 1, 3, 5, 7, 8
+
+
+def dot(a, b, dims=((1,), (0,))):
+    return lax.dot_general(a, b, (dims, ((), ())), preferred_element_type=F32)
+
+
+def split(a):
+    high = a.astype(BF16)
+    return high, (a - high.astype(F32)).astype(BF16)
 
 
 def block_masks():
@@ -40,9 +39,9 @@
 def main_kernel(
     tokens_hbm, factors_hbm, w_hbm, cot_hbm,
     proj_hbm, grad_tokens_hbm, grad_factors_hbm,
-    tokens, factors, proj, grad_factors, w_own, mats, z1, z2, p2, z3, p3, ga, gb, gc, gf, cin, gh, ghb, ain, res, fout,
+    tokens, factors, proj, grad_factors, w_own, mats, flipped, z1, z2, z3, ga, gb, gc, gf, cin, gh, ghb, ain, res, fout,
     zsend, rot, R, cotG, w_oth, bsib, bsib_in, bown, up_out, up_in, dn_out, dn_in,
-    pbuf, px_out, px_in, gsend, gin,
+    pbuf, px_kept, px_out, px_in, gsend, gin,
     loc_sem, sx, rx, sy, ry, sc, rc, sw, rw, sys, yr, sR, rR, sS, rS, sB, rB, sZ, rZ, sP, rP,
     sG, rG, sC, rC, sA, rA, sF, rF, sH, rH,
 ):
@@ -116,21 +115,38 @@
         copy.wait()
 
     masks = block_masks()
+    nothing = jnp.zeros((128, 128), BF16)
+
+    def put_matrix(place, q, stacked, mask):
+        u, k = q // 2, q % 2
+        rows, rest = pl.ds(128 * k, 128), pl.ds(128 * (1 - k), 128)
+        for part, value in enumerate(split(jnp.where(mask, stacked, 0.0))):
+            mats[part, place, u, rows, rows] = value
+            mats[part, place, u, rows, rest] = nothing
+
+    def put_cross(section, bit, own):
+        for q, cols in enumerate(Q):
+            for part, place in ((bit, own), (1 - bit, own + 1)):
+                coeffs = factors[section, pl.ds(32 * part, 32), cols]
+                put_matrix(place, q, jnp.concatenate([coeffs] * 4, 0), masks[2])
+
+    def times(parts, place, u, dims=((1,), (0,))):
+        high, low = mats[0, place, u], mats[1, place, u]
+        total = dot(parts[0], high, dims) + dot(parts[0], low, dims)
+        return total + dot(parts[1], high, dims) if len(parts) > 1 else total
+
+    def times_back(parts, place, u):
+        return times(parts, place, u, ((1,), (1,)))
+
     for q, cols in enumerate(Q):
         c0, c1 = factors[0, :, cols], factors[1, :, cols]
-        mats[M0, q] = jnp.where(masks[0], jnp.concatenate([c0, c0], 0), 0.0)
-        mats[M1, q] = jnp.where(
-            masks[1], jnp.concatenate([c1[:32], c1[:32], c1[32:], c1[32:]], 0), 0.0
-        )
-        for section, bit, own in ((2, x % 2, OWN2), (3, yl, OWN3)):
-            for part, place in ((bit, own), (1 - bit, own + 1)):
-                coeffs = factors[section, pl.ds(32 * part, 32), cols]
-                mats[place, q] = jnp.where(masks[2], jnp.concatenate([coeffs] * 4, 0), 0.0)
-    for q, cols in enumerate(Q):
-        field = tokens[:, cols].astype(F32)
-        field = field + hdot(field, mats[M0, q])
+        put_matrix(M0, q, jnp.concatenate([c0, c0], 0), masks[0])
+        put_matrix(M1, q, jnp.concatenate([c1[:32], c1[:32], c1[32:], c1[32:]], 0), masks[1])
+    for u, cols in enumerate(U):
+        field = tokens[:, cols]
+        field = field.astype(F32) + times([field], M0, u)
         z1[:, cols] = field
-        field = field + hdot(field, mats[M1, q])
+        field = field + times(split(field), M1, u)
         z2[:, cols] = field
         zsend[0, :, cols] = field.astype(BF16)
 
@@ -146,13 +162,15 @@
         n = i + (0 if to is right else 2)
         send(cot_hbm.at[pl.ds(256 * i, 256)], cotG.at[2 * x + i], sc, rc.at[n], to)
     send_w(0)
+    put_cross(2, x % 2, OWN2)
+    put_cross(3, yl, OWN3)
+    for u, cols in enumerate(U):
+        field = z2[:, cols]
+        z3[:, cols] = field + times(split(field), OWN2, u)
     for h in range(2):
         arrived(zsend.at[2, H[h]], rx.at[h])
-        for q, cols in enumerate(Q):
-            theirs = zsend[2, H[h], cols].astype(F32)
-            p2[H[h], cols] = theirs
-            field = z2[H[h], cols]
-            field = field + hdot(field, mats[OWN2, q]) + hdot(theirs, mats[OTHER2, q])
+        for u, cols in enumerate(U):
+            field = z3[H[h], cols] + times([zsend[2, H[h], cols]], OTHER2, u)
             z3[H[h], cols] = field
             zsend[1, H[h], cols] = field.astype(BF16)
         send(zsend.at[1, H[h]], zsend.at[3, H[h]], sy, ry.at[h], ypair)
@@ -164,14 +182,13 @@
         dst = R.at[z, slot, core, H[h]]
         return rcopy(src, dst, sys.at[b], yr.at[slot, h], dev(yh=b, yl=yh))
 
+    for u, cols in enumerate(U):
+        field = z3[:, cols]
+        gc[:, cols] = field + times(split(field), OWN3, u)
     for h in range(2):
         arrived(zsend.at[3, H[h]], ry.at[h])
-        for q, cols in enumerate(Q):
-            theirs = zsend[3, H[h], cols].astype(F32)
-            p3[H[h], cols] = theirs
-            field = z3[H[h], cols]
-            field = field + hdot(field, mats[OWN3, q]) + hdot(theirs, mats[OTHER3, q])
-            rot[H[h], cols] = field.astype(BF16)
+        for u, cols in enumerate(U):
+            rot[H[h], cols] = (gc[H[h], cols] + times([zsend[3, H[h], cols]], OTHER3, u)).astype(BF16)
         for b in range(2):
             pl.when(jnp.logical_not((yh == b) & diagonal))(to_holder(b, h).start)
 
@@ -232,7 +249,16 @@
         copy.wait()
     own_w.wait()
     back_unit(x, 0)
+    for saved, place in ((z1, T1), (z2, T2), (z3, T3)):
+        for cols in Q:
+            high, low = split(saved[:, cols].T)
+            flipped[place, cols] = high
+            flipped[place + 1, cols] = low
     step(1, True)
+    for cols in Q:
+        flipped[T0, cols] = tokens[:, cols].astype(F32).T.astype(BF16)
+        flipped[P2, cols] = zsend[2, :, cols].astype(F32).T.astype(BF16)
+        flipped[P3, cols] = zsend[3, :, cols].astype(F32).T.astype(BF16)
     arrived(cotG.at[2 * xl + 1], rc.at[1])
     back_unit(xl, 0)
     arrived(cotG.at[2 * xr], rc.at[2])
@@ -293,24 +319,44 @@
         away = (zz - z + 8) % 8
         return ((away >= 3) & (away <= 5)) == late
 
+    def px_place(direction, n):
+        return ((2 * xo + 1, 2 * xr, 2 * xr + 1), (2 * xo, 2 * xl + 1, 2 * xl))[direction][n]
+
+    def px_arrived(direction, n, h):
+        arrived(px_in.at[direction, n, PX[h]], rP.at[direction, 2 * n + h])
+
+    def px_post(direction, n, h, part):
+        if n == 2:
+            px_arrived(direction, 0, h)
+            part = part + px_in[direction, 0, PX[h]].astype(F32)
+        px_out[direction, n, PX[h]] = part.astype(BF16)
+        send(
+            px_out.at[direction, n, PX[h]], px_in.at[direction, n, PX[h]], sP,
+            rP.at[direction, 2 * n + h], left if direction else right,
+        )
+
     def px_send(late, n, after_far=None):
         for direction in range(2):
-            zz = ((2 * xo + 1, 2 * xr, 2 * xr + 1), (2 * xo, 2 * xl + 1, 2 * xl))[direction][n]
-            now = in_phase(zz, late)
+            now = in_phase(px_place(direction, n), late)
             if after_far is not None:
-                now = now & in_phase(2 * xo + 1 - direction, after_far)
+                now = now & in_phase(px_place(direction, 0), after_far)
 
             @pl.when(now)
             def _():
-                value = product(zz)
-                if n == 2:
-                    arrived(px_in.at[direction, 0], rP.at[direction, 0])
-                    value = value + px_in[direction, 0].astype(F32)
-                px_out[direction, n] = value.astype(BF16)
-                send(
-                    px_out.at[direction, n], px_in.at[direction, n], sP, rP.at[direction, n],
-                    left if direction else right,
-                )
+                value = product(px_place(direction, n))
+                for h in range(2):
+                    px_post(direction, n, h, value[128 * h:128 * h + 128])
+
+    def px_last(h):
+        for direction in range(2):
+            @pl.when(in_phase(px_place(direction, 2), True))
+            def _():
+                if h == 0:
+                    value = product(px_place(direction, 2))
+                    px_post(direction, 2, 0, value[:128])
+                    px_kept[direction] = value[128:]
+                else:
+                    px_post(direction, 2, 1, px_kept[direction])
 
     def px_own(late):
         for i in range(2):
@@ -353,22 +399,22 @@
     back_unit((far + 4 - turn) % 4, 1)
     third_step(0)
     back_unit((far + 2) % 4, 1)
+    px_send(False, 1)
     ring_send(1, 2)
     ring_end(0)
     back_ready(1, 2, -2)
     ring_send(1, 3)
-    px_send(False, 1)
+    px_send(False, 2)
     ring_send(1, 4)
     back_ready(1, 1, -1, 0)
     ring_send(1, 5)
     px_own(False)
     ring_send(1, 6)
+    ring_end(1)
     held = ((z_at(-2), 1, 0, 2, above), (z_at(2), 1, 1, 2, below), (z_at(-3), 0, 0, 3, above))
     for zz, s, direction, k, to in held:
         block = R.at[zz, s, core]
         send(block, block, sR.at[direction], rR.at[direction, k, s], to)
-    px_send(False, 2)
-    ring_end(1)
     third_step(1)
 
     def reduce_start(s):
@@ -411,23 +457,29 @@
         res[...] = total.astype(BF16)
         fout[core, own_s, own_rows, own_cols] = res[...]
 
-        def push(r, carry):
+        for r in (4, 12, 3, 5, 11, 13, 2, 6, 10, 14, 1, 7, 9, 15, 8):
             peer_copy(r).start()
-            return carry
-
-        lax.fori_loop(1, 16, push, 0)
 
     def cross_out(g, h, other, a, ssem, rsem, peer):
-        for q, cols in enumerate(Q):
-            zsend[a, H[h], cols] = hdot_nt(g[H[h], cols], mats[other, q]).astype(BF16)
+        for u, cols in enumerate(U):
+            zsend[a, H[h], cols] = times_back(split(g[H[h], cols]), other, u).astype(BF16)
         send(zsend.at[a, H[h]], zsend.at[a + 1, H[h]], ssem, rsem, peer)
 
+    def products_with(parts, place, u, exact):
+        total = dot(flipped[place, U[u]], parts[0]) + dot(flipped[place, U[u]], parts[1])
+        return total if exact else total + dot(flipped[place + 1, U[u]], parts[0])
+
+    def diagonals(full, u):
+        return ((full[:128, :128], Q[2 * u]), (full[128:, 128:], Q[2 * u + 1]))
+
     def cross_kept(g, out, section, own, saved, partner, bit):
-        for q, cols in enumerate(Q):
+        for u, cols in enumerate(U):
             field = g[:, cols]
-            out[:, cols] = field + hdot_nt(field, mats[own, q])
-            gf[section, pl.ds(32 * bit, 32), cols] = fold_cross(hdot_tn(saved[:, cols], field), masks)
-            gf[section, pl.ds(32 * (1 - bit), 32), cols] = fold_cross(hdot_tn(partner[:, cols], field), masks)
+            parts = split(field)
+            out[:, cols] = field + times_back(parts, own, u)
+            for place, exact, side in ((saved, False, bit), (partner, True, 1 - bit)):
+                for full, q in diagonals(products_with(parts, place, u, exact), u):
+                    gf[section, pl.ds(32 * side, 32), q] = fold_cross(full, masks)
         reduce_start(section)
 
     def cross_in(out, h, a, rsem):
@@ -435,15 +487,17 @@
         out[H[h]] += zsend[a + 1, H[h]].astype(F32)
 
     def local_back(g, out, section, saved):
-        for q, cols in enumerate(Q):
+        for u, cols in enumerate(U):
             field = g[:, cols]
-            out[:, cols] = field + hdot_nt(field, mats[section, q])
-            full = jnp.where(masks[section], hdot_tn(saved[:, cols].astype(F32), field), 0.0)
-            if section == 0:
-                gf[0, :, cols] = full[:64] + full[64:]
-            else:
-                gf[1, pl.ds(0, 32), cols] = full[:32] + full[32:64]
-                gf[1, pl.ds(32, 32), cols] = full[64:96] + full[96:]
+            parts = split(field)
+            out[:, cols] = field + times_back(parts, section, u)
+            for full, q in diagonals(products_with(parts, saved, u, section == 0), u):
+                full = jnp.where(masks[section], full, 0.0)
+                if section == 0:
+                    gf[0, :, q] = full[:64] + full[64:]
+                else:
+                    gf[1, pl.ds(0, 32), q] = full[:32] + full[32:64]
+                    gf[1, pl.ds(32, 32), q] = full[64:96] + full[96:]
         reduce_start(section)
 
     for h in range(2):
@@ -453,29 +507,30 @@
                 arrived(gin.at[a, H[h]], rG.at[a, h])
         ga[H[h]] = gin[0, H[h]].astype(F32) + gin[1, H[h]].astype(F32)
         cross_out(ga, h, OTHER3, 4, sy, ry.at[2 + h], ypair)
-    cross_kept(ga, gb, 3, OWN3, z3, p3, yl)
+    cross_kept(ga, gb, 3, OWN3, T3, P3, yl)
     last_step()
     for h in range(2):
         cross_in(gb, h, 4, ry.at[2 + h])
         cross_out(gb, h, OTHER2, 6, sx, rx.at[2 + h], xpair)
-    cross_kept(gb, gc, 2, OWN2, z2, p2, x % 2)
+    cross_kept(gb, gc, 2, OWN2, T2, P2, x % 2)
     arrived(R.at[pl.ds(0, 3), :, 0], rS.at[1])
     px_send(True, 0)
     px_send(True, 1, False)
     for h in range(2):
         cross_in(gc, h, 6, rx.at[2 + h])
     reduce_middle(3)
-    local_back(gc, gb, 1, z1)
-    local_back(gb, ga, 0, tokens)
+    local_back(gc, gb, 1, T1)
+    local_back(gb, ga, 0, T0)
     grad_tokens_out = local(ga, grad_tokens_hbm, 5)
     grad_tokens_out.start()
     reduce_middle(2)
     reduce_middle(1)
     reduce_middle(0)
+    px_last(0)
     px_send(True, 1, True)
     pl.when(own_s >= 2)(own_work)
-    px_send(True, 2)
     pl.when(own_s < 2)(own_work)
+    px_last(1)
     px_own(True)
     for s in (3, 2, 1, 0):
         @pl.when(own_s != s)
@@ -495,8 +550,9 @@
         factors_out[s].start()
 
     for i, nu, nd in ((0, 1, 2), (1, 2, 1)):
-        arrived(px_in.at[0, nu], rP.at[0, nu])
-        arrived(px_in.at[1, nd], rP.at[1, nd])
+        for h in range(2):
+            px_arrived(0, nu, h)
+            px_arrived(1, nd, h)
         total = pbuf[i] + px_in[0, nu].astype(F32) + px_in[1, nd].astype(F32)
         proj[pl.ds(256 * i, 256), :] = total.astype(BF16)
 
@@ -543,8 +599,9 @@
             V((512, 896), BF16),
             V((4, 64, 768), F32),
             V((768, 896), BF16),
-            V((6, 6, 128, 128), F32),
-            *[V((128, 768), F32)] * 8,
+            V((2, 6, 3, 256, 256), BF16),
+            V((9, 768, 128), BF16),
+            *[V((128, 768), F32)] * 6,
             V((4, 64, 768), F32),
             V((4, 32, 768), F32),
             V((4, 32, 768), F32),
@@ -562,6 +619,7 @@
             V((8, 2, 128, 768), F32),
             *[V((14, 64, 768), BF16)] * 4,
             V((2, 256, 896), F32),
+            V((2, 128, 896), F32),
             V((2, 3, 256, 896), BF16),
             V((2, 3, 256, 896), BF16),
             V((2, 128, 768), BF16),
@@ -574,7 +632,7 @@
             D, D((2,)),
             D, D((8, 2)),
             D((2,)), D((2, 14)),
-            D, D((2, 3)),
+            D, D((2, 6)),
             D((2,)), D((2, 2)),
             D, D((4,)),
             D, D,
@@ -582,7 +640,7 @@
             D, D((4,)),
         ],
         compiler_params=pltpu.CompilerParams(
-            collective_id=0, has_side_effects=True, vmem_limit_bytes=56 * 1024 * 1024
+            collective_id=0, has_side_effects=True, vmem_limit_bytes=60 * 1024 * 1024
         ),
         name="rotate_project",
     )(tokens, factors, weight, cotangent)

time: 126 us -> 124 us (0.984)
  Pallas kernels: 122 us -> 119 us
    pallas_call x1, Pallas kernels: 122 us -> 119 us  [per_device(): pl.pallas_call(main_kernel, out_shape=shapes, in_specs=[hbm] * 4, out_spe...]
where the time goes in v5:
time: 124 us; the launch traced here: 123 us
  Pallas kernels  119 us (96%)
  local copies, waits for them, and re-layouts  3.9 us (3%)
    pallas_call x1, Pallas kernels, per_device(): pl.pallas_call(main_kernel, out_shape=shapes, in_specs=[hbm] * 4, out_spe...  119 us
    unnamed x7, local copies, waits for them, and re-layouts  3.9 us

profile of v5, /device:TPU:1, one launch (start us, length us, event | category | flops | bytes accessed | tf_op | source)
XLA Modules:
  0.0 123.3 jit_solution(10042365375550250516)
XLA Ops:
  0.6 118.8 %rotate_project.1 = (bf16[512,896]{1,0:T(8,128)(2,1)}, f32[128,768]{1,0:T(8,128)}, f32[4,64,768]{2,1,0:T(8,128)}) custom-call(bf16[128,768]{1,0:T(8,128)(2,1)} %tokens_hbm.1, f32[4,64,768]{2,1,0:T(8,128)} %factors_hbm.1, bf16[768,896]{1,0:T(8,128)(2,1)} %w_hbm.1, bf16[512,896]{1,0:T(8,128)(2,1)} %cot_hbm.1), custom_call_target="tpu_custom_call" | custom-call | tf_op jit(solution)/shard_map/rotate_project/pallas_call | solution.py:591
  119.4 0.0 copy-start.1
  119.4 0.0 copy-start
  119.4 2.3 %copy.10 = bf16[512,896]{1,0:T(8,128)(2,1)} copy(bf16[512,896]{1,0:T(8,128)(2,1)} %get-tuple-element.6) | data formatting | bytes 1835008
  121.7 0.0 copy-done.1
  121.7 0.7 copy.11
  122.5 0.0 copy-done
  122.5 0.9 copy.12
Async XLA Ops:
  119.4 2.3 %copy-start.1 = (f32[128,768]{1,0:T(8,128)S(1)}, f32[128,768]{1,0:T(8,128)}, u32[]{:S(2)}) copy-start(f32[128,768]{1,0:T(8,128)} %get-tuple-element.7) | copy-start | bytes 1179652
  119.4 3.0 %copy-start = (f32[4,64,768]{2,1,0:T(8,128)S(1)}, f32[4,64,768]{2,1,0:T(8,128)}, u32[]{:S(2)}) copy-start(f32[4,64,768]{2,1,0:T(8,128)} %get-tuple-element.8) | copy-start | bytes 2359300

commit v6 on v5

--- a/solution.py
+++ b/solution.py
@@ -579,6 +579,21 @@
     all_sent(fout.at[0], sH)
 
 
+def hand_over(proj, grad_tokens, grad_factors, proj_out, tokens_out, factors_out, a, b, c, came, gone):
+    parts = [(proj, a, proj_out, pl.ds(128 * i, 128)) for i in range(4)]
+    parts += [(grad_factors, c, factors_out, i) for i in range(4)]
+    parts.append((grad_tokens, b, tokens_out, pl.ds(0, 128)))
+    into = [pltpu.make_async_copy(s.at[i], v.at[i], came.at[n]) for n, (s, v, d, i) in enumerate(parts)]
+    out = [pltpu.make_async_copy(v.at[i], d.at[i], gone.at[n]) for n, (s, v, d, i) in enumerate(parts)]
+    for copy in into:
+        copy.start()
+    for first, second in zip(into, out):
+        first.wait()
+        second.start()
+    for copy in out:
+        copy.wait()
+
+
 def per_device(tokens, weight, factors, cotangent):
     V = pltpu.VMEM
     D = pltpu.SemaphoreType.DMA
@@ -588,7 +603,7 @@
         jax.ShapeDtypeStruct((4, 64, 768), F32),
     )
     hbm = pl.BlockSpec(memory_space=pl.ANY)
-    return pl.pallas_call(
+    results = pl.pallas_call(
         main_kernel,
         out_shape=shapes,
         in_specs=[hbm] * 4,
@@ -644,6 +659,21 @@
         ),
         name="rotate_project",
     )(tokens, factors, weight, cotangent)
+    return pl.pallas_call(
+        hand_over,
+        out_shape=shapes,
+        in_specs=[hbm] * 3,
+        out_specs=(hbm,) * 3,
+        scratch_shapes=[
+            V((512, 896), BF16),
+            V((128, 768), F32),
+            V((4, 64, 768), F32),
+            D((9,)),
+            D((9,)),
+        ],
+        compiler_params=pltpu.CompilerParams(vmem_limit_bytes=62 * 1024 * 1024),
+        name="hand_over",
+    )(*results)
 
 
 def solution(mesh):

time: 124 us -> 123 us (level)
  local copies, waits for them, and re-layouts: 3.9 us -> 0 us
  Pallas kernels: 119 us -> 121 us
    unnamed x7 -> x0, local copies, waits for them, and re-layouts: 3.9 us -> none
    pallas_call x0 -> x1, Pallas kernels: none -> 2.55 us  [per_device(): pl.pallas_call(hand_over, out_shape=shapes, in_specs=[hbm] * 3, out_specs...]
where the time goes in v6:
time: 123 us; the launch traced here: 122 us
  Pallas kernels  121 us (98%)
    pallas_call x1, Pallas kernels, per_device(): pl.pallas_call(main_kernel, out_shape=shapes, in_specs=[hbm] * 4, out_spe...  119 us
    pallas_call x1, Pallas kernels, per_device(): pl.pallas_call(hand_over, out_shape=shapes, in_specs=[hbm] * 3, out_specs...  2.55 us

profile of v6, /device:TPU:1, one launch (start us, length us, event | category | flops | bytes accessed | tf_op | source)
XLA Modules:
  0.0 122.2 jit_solution(17443931119478153111)
XLA Ops:
  0.6 118.8 %rotate_project.1 = (bf16[512,896]{1,0:T(8,128)(2,1)}, f32[128,768]{1,0:T(8,128)}, f32[4,64,768]{2,1,0:T(8,128)}) custom-call(bf16[128,768]{1,0:T(8,128)(2,1)} %tokens_hbm.1, f32[4,64,768]{2,1,0:T(8,128)} %factors_hbm.1, bf16[768,896]{1,0:T(8,128)(2,1)} %w_hbm.1, bf16[512,896]{1,0:T(8,128)(2,1)} %cot_hbm.1), custom_call_target="tpu_custom_call" | custom-call | tf_op jit(solution)/shard_map/rotate_project/pallas_call | solution.py:606
  119.4 2.5 %hand_over.1 = (bf16[512,896]{1,0:T(8,128)(2,1)}, f32[128,768]{1,0:T(8,128)}, f32[4,64,768]{2,1,0:T(8,128)}) custom-call(bf16[512,896]{1,0:T(8,128)(2,1)} %get-tuple-element.6.proj, f32[128,768]{1,0:T(8,128)} %get-tuple-element.7.grad_tokens, f32[4,64,768]{2,1,0:T(8,128)} %get-tuple-element.8.grad_factors), custom_call_target="tpu_custom_call" | custom-call | tf_op jit(solution)/shard_map/hand_over/pallas_call | solution.py:662

commit v7 on v6

--- a/solution.py
+++ b/solution.py
@@ -415,7 +415,7 @@
     for zz, s, direction, k, to in held:
         block = R.at[zz, s, core]
         send(block, block, sR.at[direction], rR.at[direction, k, s], to)
-    third_step(1)
+    pl.when(off_diagonal)(lambda: third_step(1))
 
     def reduce_start(s):
         send(gf.at[s, pl.ds(32 * (1 - core), 32)], cin.at[s], sC, rC.at[s], sibling)
@@ -508,6 +508,7 @@
         ga[H[h]] = gin[0, H[h]].astype(F32) + gin[1, H[h]].astype(F32)
         cross_out(ga, h, OTHER3, 4, sy, ry.at[2 + h], ypair)
     cross_kept(ga, gb, 3, OWN3, T3, P3, yl)
+    pl.when(diagonal)(lambda: third_step(1))
     last_step()
     for h in range(2):
         cross_in(gb, h, 4, ry.at[2 + h])
@@ -529,8 +530,8 @@
     px_last(0)
     px_send(True, 1, True)
     pl.when(own_s >= 2)(own_work)
+    px_last(1)
     pl.when(own_s < 2)(own_work)
-    px_last(1)
     px_own(True)
     for s in (3, 2, 1, 0):
         @pl.when(own_s != s)

time: 123 us -> 123 us (level)
  no operation moved by 1% of the time
where the time goes in v7:
time: 123 us; the launch traced here: 122 us
  Pallas kernels  121 us (98%)
    pallas_call x1, Pallas kernels, per_device(): pl.pallas_call(main_kernel, out_shape=shapes, in_specs=[hbm] * 4, out_spe...  119 us
    pallas_call x1, Pallas kernels, per_device(): pl.pallas_call(hand_over, out_shape=shapes, in_specs=[hbm] * 3, out_specs...  2.55 us

profile of v7, /device:TPU:1, one launch (start us, length us, event | category | flops | bytes accessed | tf_op | source)
XLA Modules:
  0.0 122.2 jit_solution(17193086703370975290)
XLA Ops:
  0.6 118.8 %rotate_project.1 = (bf16[512,896]{1,0:T(8,128)(2,1)}, f32[128,768]{1,0:T(8,128)}, f32[4,64,768]{2,1,0:T(8,128)}) custom-call(bf16[128,768]{1,0:T(8,128)(2,1)} %tokens_hbm.1, f32[4,64,768]{2,1,0:T(8,128)} %factors_hbm.1, bf16[768,896]{1,0:T(8,128)(2,1)} %w_hbm.1, bf16[512,896]{1,0:T(8,128)(2,1)} %cot_hbm.1), custom_call_target="tpu_custom_call" | custom-call | tf_op jit(solution)/shard_map/rotate_project/pallas_call | solution.py:607
  119.4 2.5 %hand_over.1 = (bf16[512,896]{1,0:T(8,128)(2,1)}, f32[128,768]{1,0:T(8,128)}, f32[4,64,768]{2,1,0:T(8,128)}) custom-call(bf16[512,896]{1,0:T(8,128)(2,1)} %get-tuple-element.6.proj, f32[128,768]{1,0:T(8,128)} %get-tuple-element.7.grad_tokens, f32[4,64,768]{2,1,0:T(8,128)} %get-tuple-element.8.grad_factors), custom_call_target="tpu_custom_call" | custom-call | tf_op jit(solution)/shard_map/hand_over/pallas_call | solution.py:663
